TPU v7x, 128 devices: a whole 4x4x4 slice. The times are simulated.
128 devices in a mesh: section: 4 (over z_lo, core), dp: 32 (over z_hi, x, y).
Axes of the slice: x: 4, y: 4, z: 4 (z_hi: 2, z_lo: 2; z = z_hi * 2 + z_lo), core: 2. Of those that a mesh axis runs over, the one named last changes fastest.
Arguments:
- latents: bfloat16 [2, 32, 128, 3072], P(None, 'dp'), may hold values from -6 to 6
- modulation: float32 [4, 2, 32, 3, 3072], P('section', None, 'dp'), may hold values from -2 to 2
- query_key_value_weight: bfloat16 [4, 3072, 4608], P('section', None, 'dp'), may hold values from -0.109375 to 0.109375
- output_projection_weight: bfloat16 [4, 1536, 3072], P('section', None, 'dp'), may hold values from -0.15625 to 0.15625
- positions: int32 [2, 32, 128], P(None, 'dp'), may hold values from 0 to 4095, as said below
- counts: int32 [2, 32], P(None, 'dp'), may hold values from 1 to 128, as said below
Outputs:
- stash: bfloat16 [4, 2, 32, 128, 3072], P('section', None, 'dp')
Inputs may be any that keep to these rules, and one draw needn't show every extreme that they name: Within a sample all 128 positions are distinct. `counts`: sample 0 of every microbatch uses all 128 slots.
All inputs are finite; a program needn't handle non-finite values.
Results may differ from a plain program's by a relative error of at most 0.039.
Values may be sent and summed in bfloat16 or wider, within the bound.
No kernel may reach another device: no remote copies, remote signals or barrier semaphores. Data moves between devices by JAX's collectives and lax.ppermute only.
A program may use at most 128 MiB of HBM per device.

v0:
```python
import functools

import jax
import jax.numpy as jnp
from jax import lax
from jax.experimental import pallas as pl
from jax.experimental.pallas import tpu as pltpu
from jax.sharding import Mesh
from jax.sharding import PartitionSpec as P

D = 3072
HEADS = 12
HSZ = 128
GRID = 64
TOK = 128
HD = 1536
LAYERS = 4
ROWS = 2 * TOK
QD = D // 4
QH = HD // 4
AXES = ("z_lo", "core", "z_hi", "x", "y")
VMEM_LIMIT = 48 * 1024 * 1024
HBM = pl.BlockSpec(memory_space=pl.ANY)
SMEM = pl.BlockSpec(memory_space=pltpu.SMEM)
VMEM = pl.BlockSpec(memory_space=pltpu.VMEM)


def device_permute(value, place):
    pairs = []
    for z in range(4):
        for c in range(2):
            target = place(z, c)
            if target is not None:
                tz, tc = target
                pairs.append(((z % 2) * 4 + c * 2 + z // 2, (tz % 2) * 4 + tc * 2 + tz // 2))
    return lax.ppermute(value, ("z_lo", "core", "z_hi"), pairs)


def ring_step(value, steps):
    return device_permute(value, lambda z, c: ((z + steps) % 4, c))


def ring_gather(value):
    return [value] + [ring_step(value, k) for k in (1, 2, 3)]


def ring_gather_rows(first, second):
    first_before, second_after = ring_step(first, 1), ring_step(second, 3)
    second_before, first_after = ring_step(second, 1), ring_step(first, 3)
    return [first, second, first_before, second_before, first_after, second_after, ring_step(first_before, 1), ring_step(second_after, 3)]


def core_swap(value):
    return lax.ppermute(value, "core", [(0, 1), (1, 0)])


def rotate(values, cosine, sine, first):
    partner = jnp.where(first, pltpu.roll(values, 96, 1), pltpu.roll(values, 32, 1))
    return (values * cosine + partner * sine).astype(jnp.bfloat16)


def attention_kernel(first, keeps, last, meta, *rest):
    states, (mods, cosine, sine, weights), outs, (w, y, both, sems, keep_sem) = rest[:8], rest[8:12], rest[12:-5], rest[-5:]
    if keeps:
        kept = outs[-1]
        for b in range(2):

            @pl.when(meta[6] == b)
            def keep(pieces=states[b::2]):
                for k, p in enumerate(pieces):
                    place = pl.ds(pl.multiple_of(meta[k] * QD, QD), QD)
                    pltpu.make_async_copy(p, kept.at[:, place], keep_sem).start()

    for i in range(4):
        core, plane = i // 2, pl.ds(i % 2 * 8, 8)
        for j in range(3):
            source = weights.at[core, plane, :, pl.ds(first + 48 * j, 48), :]
            pltpu.make_async_copy(source, w.at[i, :, :, :, pl.ds(QH * j, QH)], sems.at[i]).start()
    for b in range(2):
        rows = pl.ds(b * TOK, TOK)
        pieces = states[b::2]
        total = jnp.zeros((TOK, 1), jnp.float32)
        for p in pieces:
            total += jnp.sum(p[...].astype(jnp.float32), axis=1, keepdims=True)
        center = total / D
        total = jnp.zeros((TOK, 1), jnp.float32)
        for p in pieces:
            total += jnp.sum((p[...].astype(jnp.float32) - center) ** 2, axis=1, keepdims=True)
        inverse = 1.0 / jnp.sqrt(total / D + 1e-06)
        for k, p in enumerate(pieces):
            q = meta[k]
            normed = (p[...].astype(jnp.float32) - center) * inverse
            shift = mods[q, b, 0:1, :]
            scale = mods[q, b, 1:2, :]
            y[rows, pl.ds(pl.multiple_of(q * QD, QD), QD)] = (normed * (1.0 + scale) + shift).astype(jnp.bfloat16)

    total = jnp.zeros((ROWS, 3 * QH), jnp.float32)
    for i in range(4):
        pltpu.make_async_copy(w.at[i], w.at[i], sems.at[i]).wait()
        total += jnp.dot(y[:, i * QD : (i + 1) * QD], w[i].reshape(QD, 3 * QH), preferred_element_type=jnp.float32)
    qkv = total.astype(jnp.bfloat16)
    lane = lax.broadcasted_iota(jnp.int32, (TOK, HSZ), 1)
    first = (lane % 64) < 32
    for b in range(2):
        live = lane < meta[4 + b]
        lo = b * TOK
        cb, sb = cosine[lo : lo + TOK, :], sine[lo : lo + TOK, :]
        for h in range(3):
            query = rotate(qkv[lo : lo + TOK, h * HSZ : (h + 1) * HSZ].astype(jnp.float32), cb, sb, first)
            key = rotate(qkv[lo : lo + TOK, QH + h * HSZ : QH + (h + 1) * HSZ].astype(jnp.float32), cb, sb, first)
            value = qkv[lo : lo + TOK, 2 * QH + h * HSZ : 2 * QH + (h + 1) * HSZ]
            scores = lax.dot_general(query, key, (((1,), (1,)), ((), ())), preferred_element_type=jnp.float32)
            scores = jnp.where(live, scores * HSZ ** (-0.5), -1e30)
            expd = jnp.exp(scores - jnp.max(scores, axis=1, keepdims=True))
            weights = (expd / jnp.sum(expd, axis=1, keepdims=True)).astype(jnp.bfloat16)
            mixed = jnp.dot(weights, value, preferred_element_type=jnp.float32)
            mixed = mixed.astype(jnp.bfloat16)
            cols = pl.ds(h * HSZ, HSZ)
            if last:
                both[b, :, cols] = mixed
            else:
                outs[0][lo : lo + TOK, cols] = mixed
    if last:
        outs[0][...] = both[meta[6]]
        outs[1][...] = both[1 - meta[6]]
    if keeps:
        pltpu.make_async_copy(kept, kept, keep_sem).wait()


def fetch_kernel(start, weights, out, sem):
    copy = pltpu.make_async_copy(weights.at[:, :, :, pl.ds(start, 48), :], out, sem)
    copy.start()
    copy.wait()


def fetch(weights, start, after):
    weights, _ = lax.optimization_barrier((weights, after))
    return pl.pallas_call(
        functools.partial(fetch_kernel, start),
        out_shape=jax.ShapeDtypeStruct((2, 16, 2, 48, QH), jnp.bfloat16),
        in_specs=[HBM],
        out_specs=VMEM,
        scratch_shapes=[pltpu.SemaphoreType.DMA],
        compiler_params=pltpu.CompilerParams(vmem_limit_bytes=VMEM_LIMIT),
        cost_estimate=pl.CostEstimate(flops=0, bytes_accessed=5000000, transcendentals=0),
        name="fetch",
    )(weights)


def project_kernel(meta, a0, a1, a2, a3, hidden0, hidden1, gate, w, out0, out1, a):
    for k, part in enumerate((a0, a1, a2, a3)):
        a[:, pl.ds(pl.multiple_of(meta[7 + k] * QH, QH), QH)] = part[...]
    for n in range(2):
        cols = pl.ds(n * QH, QH)
        proj = jnp.dot(a[...], w[n].reshape(HD, QH), preferred_element_type=jnp.float32).astype(jnp.bfloat16)
        for b, (hidden, out) in enumerate(((hidden0, out0), (hidden1, out1))):
            change = gate[b : b + 1, cols] * proj[b * TOK : (b + 1) * TOK, :].astype(jnp.float32)
            out[:, cols] = (hidden[:, cols].astype(jnp.float32) + change).astype(jnp.bfloat16)


def finish_kernel(meta, a0, a1, a2, a3, *rest):
    states, (gate, weights, kept1, kept2, stay, leave, w, a, early, sems) = rest[:8], rest[8:]
    copies = []
    for k, ring in enumerate((0, 1, 3, 2)):
        copies.append(pltpu.make_async_copy(weights.at[:, :, :, pl.ds(ring * 48, 48), :], w.at[k], sems.at[k]))
        copies[-1].start()
    for z_lo, kept in enumerate((kept1, kept2)):

        @pl.when(meta[11] == z_lo)
        def bring(kept=kept):
            pltpu.make_async_copy(kept, early, sems.at[4]).start()

    for k, part in enumerate((a0, a1, a2, a3)):
        a[:, pl.ds(pl.multiple_of(meta[7 + k] * QH, QH), QH)] = part[...]
    pltpu.make_async_copy(kept1, early, sems.at[4]).wait()
    b = meta[6]
    for k in range(4):
        copies[k].wait()
        q = meta[k]
        for n in range(2):
            cols = pl.ds(n * QH, QH)
            proj = jnp.dot(a[...], w[k, n].reshape(HD, QH), preferred_element_type=jnp.float32).astype(jnp.bfloat16)
            hidden = jnp.where(b == 0, states[2 * k][:, cols], states[2 * k + 1][:, cols])
            change = gate[q, pl.ds(b, 1), cols] * proj.astype(jnp.float32)
            place = pl.ds(pl.multiple_of(q * QD + n * QH, QH), QH)
            late = jnp.where(meta[11] == 0, (hidden.astype(jnp.float32) + change).astype(jnp.bfloat16), hidden)
            stay[:, place] = jnp.where(meta[11] == meta[12], late, early[:, place])
            leave[:, place] = jnp.where(meta[11] == meta[12], early[:, place], late)


def attention(meta, pieces, mods, cosine, sine, weights, first, keeps, last):
    if last:
        attended = (jax.ShapeDtypeStruct((TOK, QH), jnp.bfloat16),) * 2
    else:
        attended = (jax.ShapeDtypeStruct((ROWS, QH), jnp.bfloat16),)
    return pl.pallas_call(
        functools.partial(attention_kernel, first, keeps, last),
        out_shape=attended + (jax.ShapeDtypeStruct((TOK, D), jnp.bfloat16),) * keeps,
        in_specs=[SMEM] + [VMEM] * 11 + [HBM],
        out_specs=(VMEM,) * len(attended) + (HBM,) * keeps,
        scratch_shapes=[
            pltpu.VMEM((4, 8, 2, 48, 3 * QH), jnp.bfloat16),
            pltpu.VMEM((ROWS, D), jnp.bfloat16),
            pltpu.VMEM((2, TOK, QH), jnp.bfloat16),
            pltpu.SemaphoreType.DMA((4,)),
            pltpu.SemaphoreType.DMA,
        ],
        compiler_params=pltpu.CompilerParams(vmem_limit_bytes=VMEM_LIMIT),
        cost_estimate=pl.CostEstimate(flops=2 * ROWS * D * 3 * QH, bytes_accessed=10000000, transcendentals=100000),
        name="attention",
    )(meta, *pieces, mods, cosine, sine, weights)


def project(meta, parts, hidden, gate, weights):
    return pl.pallas_call(
        project_kernel,
        out_shape=(jax.ShapeDtypeStruct((TOK, QD), jnp.bfloat16),) * 2,
        in_specs=[SMEM] + [VMEM] * 8,
        out_specs=(VMEM, VMEM),
        scratch_shapes=[pltpu.VMEM((ROWS, HD), jnp.bfloat16)],
        compiler_params=pltpu.CompilerParams(vmem_limit_bytes=VMEM_LIMIT),
        cost_estimate=pl.CostEstimate(flops=2 * ROWS * HD * QD, bytes_accessed=4000000, transcendentals=0),
        name="project",
    )(meta, *parts, *hidden, gate, weights)


def finish(meta, parts, pieces, gate, weights, kept):
    return pl.pallas_call(
        finish_kernel,
        out_shape=(jax.ShapeDtypeStruct((TOK, D), jnp.bfloat16),) * 2,
        in_specs=[SMEM] + [VMEM] * 13 + [HBM] * 3,
        out_specs=(VMEM, VMEM),
        scratch_shapes=[
            pltpu.VMEM((4, 2, 16, 2, 48, QH), jnp.bfloat16),
            pltpu.VMEM((TOK, HD), jnp.bfloat16),
            pltpu.VMEM((TOK, D), jnp.bfloat16),
            pltpu.SemaphoreType.DMA((5,)),
        ],
        compiler_params=pltpu.CompilerParams(vmem_limit_bytes=VMEM_LIMIT),
        cost_estimate=pl.CostEstimate(flops=2 * TOK * HD * D, bytes_accessed=13000000, transcendentals=0),
        name="finish",
    )(meta, *parts, *pieces, gate, weights, *kept)


def pick(options, index):
    return lax.dynamic_index_in_dim(jnp.asarray(options), index, 0, keepdims=False)


def pack_kernel(qkv, outs, packed):
    qkv, outs = qkv[...].T, outs[...].T
    for d in range(32):
        z_hi, plane = d // 16, d % 16
        first, second, last = (2 * plane + z_hi) * 48, (2 * plane + z_hi + 32) * 48, (2 * plane + z_hi) * 48
        packed[d] = jnp.concatenate([qkv[first : first + 48], qkv[second : second + 48], outs[last : last + 48]], axis=1)


def regroup_kernel(mixed, blocks):
    outs = jnp.concatenate([mixed[d, :, 288:384] for d in range(32)], axis=1)
    for c in range(2):
        rows = jnp.concatenate([mixed[d, :, 144 * c : 144 * c + 144] for d in range(32)], axis=1)
        for z in range(4):
            target = (z % 2) * 4 + c * 2 + z // 2
            for j in range(3):
                blocks[target, 48 * j : 48 * j + 48, :] = rows[:, HD * j + QH * z : HD * j + QH * (z + 1)]
            blocks[target, 144:, :] = outs[:, QD * z + QH * c : QD * z + QH * (c + 1)]


def weight_shards(qkv_w, out_w):
    params = pltpu.CompilerParams(vmem_limit_bytes=VMEM_LIMIT)
    packed = pl.pallas_call(
        pack_kernel,
        out_shape=jax.ShapeDtypeStruct((32, 48, 384), jnp.bfloat16),
        compiler_params=params,
        name="pack",
    )(qkv_w.T, out_w.T)
    mixed = lax.all_to_all(packed, ("z_hi", "x", "y"), 0, 0)
    blocks = pl.pallas_call(
        regroup_kernel,
        out_shape=jax.ShapeDtypeStruct((8, 192, QH), jnp.bfloat16),
        compiler_params=params,
        name="regroup",
    )(mixed)
    shards = lax.all_to_all(blocks, ("z_lo", "core", "z_hi"), 0, 0)
    return shards.reshape(LAYERS, 2, 192, QH)


def on_device(latents, modulation, qkv_w, out_w, positions, counts):
    z_lo, core, z_hi = (lax.axis_index(a) for a in ("z_lo", "core", "z_hi"))
    z = 2 * z_hi + z_lo

    small = jnp.zeros((2, 1, D), jnp.float32)
    small = lax.dynamic_update_slice(small, positions.astype(jnp.float32).reshape(2, 1, TOK), (0, 0, 0))
    small = lax.dynamic_update_slice(small, counts.astype(jnp.float32).reshape(2, 1, 1), (0, 0, TOK))
    cond = jnp.concatenate([modulation[0, :, 0], small], axis=1)
    mine = lax.dynamic_index_in_dim(cond, core, 0, keepdims=False)
    theirs = core_swap(lax.dynamic_index_in_dim(cond, 1 - core, 0, keepdims=False))
    pair = jnp.where(core == 0, jnp.stack([mine, theirs]), jnp.stack([theirs, mine]))
    places = [(z - k) % 4 for k in range(4)]
    ring = jnp.stack(ring_gather(pair))
    by_z = [pick(ring, (z - i) % 4) for i in range(4)]
    cond = jnp.stack([jnp.stack([by_z[layer // 2][layer % 2], by_z[2 + layer // 2][layer % 2]]) for layer in range(4)])
    place = cond[0, :, 3, :TOK]
    count = cond[0, :, 3, TOK].astype(jnp.int32)
    mods = cond[:, :, 0:2].reshape(4, 2, 2, 4, QD).transpose(0, 3, 1, 2, 4)
    gates = lax.dynamic_slice_in_dim(cond[:3, :, 2], z * QD, QD, 2)
    last_gate = cond[3, :, 2].reshape(2, 4, QD).transpose(1, 0, 2)

    patch = place.astype(jnp.int32).reshape(ROWS)
    quarter = HSZ // 4
    frequency = 10000.0 ** (-jnp.arange(quarter, dtype=jnp.float32) / quarter)
    row_angle = (patch // GRID).astype(jnp.float32)[:, None] * frequency
    col_angle = (patch % GRID).astype(jnp.float32)[:, None] * frequency
    angle = jnp.concatenate([row_angle, row_angle, col_angle, col_angle], axis=1)
    cosine = jnp.cos(angle)
    sine = jnp.sin(angle) * jnp.where(jnp.arange(HSZ) % 64 < 32, -1.0, 1.0).astype(jnp.float32)

    own = lax.dynamic_index_in_dim(latents, core, 0, keepdims=False)[0]
    other = device_permute(own, lambda a, c: (3 - a, c))
    samples = (jnp.where(z_hi == 0, own, other), jnp.where(z_hi == 0, other, own))
    pieces = [sample[:, q * QD : (q + 1) * QD] for q in range(4) for sample in samples]
    quarter_of = [lax.dynamic_slice_in_dim(sample, z * QD, QD, 1) for sample in samples]

    shards = weight_shards(qkv_w[0], out_w[0])
    plane = ("core", "x", "y")
    front = lax.all_gather(jnp.concatenate([shards[0], shards[1]], axis=1), plane)
    middle = lax.all_gather(jnp.concatenate([shards[2], shards[3, :, :144]], axis=1), plane)
    across = jnp.concatenate(ring_gather(shards[3, :, 144:]), axis=1)
    final = lax.all_gather(across, plane)
    front, middle = front.reshape(2, 16, 2, 384, QH), middle.reshape(2, 16, 2, 336, QH)
    final = final.reshape(2, 16, 2, 192, QH)
    weights = [(front, 0), (front, 192), (middle, 0), (middle, 192)]
    order = [0, 1, 2, 3]
    kept = []
    for layer in range(LAYERS):
        meta = jnp.stack([jnp.asarray(v, jnp.int32) for v in order + [count[0], count[1], z_hi] + places + [z_lo, core]])
        gathered, first = weights[layer]
        att = attention(meta, pieces, mods[layer], cosine, sine, gathered, first, layer in (1, 2), layer == LAYERS - 1)
        if layer in (1, 2):
            *att, keep = att
            kept.append(keep)
        if layer < LAYERS - 1:
            quarter_of = project(meta, ring_gather(att[0]), quarter_of, gates[layer], fetch(gathered, first + 144, att[0]))
            pieces = ring_gather_rows(*quarter_of)
            order = [z, (z + 3) % 4, (z + 1) % 4, (z + 2) % 4]

    same, cross = att
    moves = [(cross, {1: 2, 3: 0}), (cross, {0: 2, 2: 0}), (same, {1: 0, 3: 2})]
    parts = [same] + [device_permute(value, lambda a, c: (move[a], c) if a in move else None) for value, move in moves]
    stay, leave = finish(meta, parts, pieces, last_gate, final, kept)
    leave = core_swap(leave)
    first = jnp.where(core == 0, stay, leave)
    second = jnp.where(core == 0, leave, stay)
    return jnp.stack([first, second])[None, :, None]


def solution(mesh):
    ring_mesh = Mesh(mesh.devices.reshape(2, 2, 2, 4, 4), AXES)
    section, dp = ("z_lo", "core"), ("z_hi", "x", "y")
    return jax.shard_map(
        on_device,
        mesh=ring_mesh,
        in_specs=(
            P(None, dp, None, None),
            P(section, None, dp, None, None),
            P(section, None, dp),
            P(section, None, dp),
            P(None, dp, None),
            P(None, dp),
        ),
        out_specs=P(section, None, dp, None, None),
        check_vma=False,
    )
```

profile of v0, /device:TPU:1, one launch (start us, length us, event | category | flops | bytes accessed | tf_op | source)
XLA Modules:
  0.0 285.7 jit_solution(7983897713323524376)
XLA Ops:
  9.6 30.4 %all_to_all.10.mixed = bf16[32,48,384]{2,1,0:T(8,128)(2,1)S(1)} all-to-all(bf16[32,48,384]{2,1,0:T(8,128)(2,1)S(1)} %pack.1), channel_id=1, replica_groups=mesh['z_lo'=2,'core'=2,'z_hi'=2,'x'=4,'y'=4] {'z_hi','x','y'}, dimensions={0} | all-to-all | bytes 2359296 | tf_op jit(solution)/shard_map/all_to_all | solution.py:276
  40.5 21.0 %all_to_all.11 = bf16[8,192,384]{2,1,0:T(8,128)(2,1)S(1)} all-to-all(bf16[8,192,384]{2,1,0:T(8,128)(2,1)S(1)} %regroup.1), channel_id=1, replica_groups=mesh['z_lo'=2,'core'=2,'z_hi'=2,'x'=4,'y'=4] {'z_lo','core','z_hi'}, dimensions={0} | all-to-all | bytes 2359296 | tf_op jit(solution)/shard_map/all_to_all | solution.py:283
  66.4 2.4 collective-permute-done.35
  73.9 2.3 collective-permute-start.4
  79.7 19.1 %collective-permute-done.1 = f32[2,4,3072]{2,1,0:T(4,128)S(1)} collective-permute-done((f32[2,4,3072]{2,1,0:T(4,128)S(1)}, f32[2,4,3072]{2,1,0:T(4,128)S(1)}, u32[]{:S(2)}, u32[]{:S(2)}) %collective-permute-start.1) | collective-permute-done | bytes 98336 | tf_op jit(solution)/shard_map/ppermute | solution.py:36
  103.7 33.0 %all-gather.7.cloned.1.call-done = bf16[64,384,384]{2,1,0:T(8,128)(2,1)} async-done(((bf16[2,384,384]{2,1,0:T(8,128)(2,1)}), bf16[64,384,384]{2,1,0:T(8,128)(2,1)}) %all-gather.7.cloned.1.call-update) | async-done | bytes 18874384 | tf_op jit(solution)/shard_map/all_gather | solution.py:325
  136.7 6.9 %attention.4.a0 = bf16[256,384]{1,0:T(8,128)(2,1)S(1)} custom-call(s32[13]{0:T(128)S(1)} %stack.166.meta, bf16[128,768]{1,0:T(8,128)(2,1)S(1)} %get-tuple-element.79.rest_0_, bf16[128,768]{1,0:T(8,128)(2,1)S(1)} %get-tuple-element.50.rest_1_, bf16[128,768]{1,0:T(8,128)(2,1)S(1)} %get-tuple-element.80.rest_2_, ...), custom_call_target="tpu_custom_call" | custom-call | flops 1811939328 | bytes 10000000 | tf_op jit(solution)/shard_map/attention/pallas_call | solution.py:196
  144.9 2.6 collective-permute-start.6
  151.1 5.4 %collective-permute-done.6.a2 = bf16[256,384]{1,0:T(8,128)(2,1)S(1)} collective-permute-done((bf16[256,384]{1,0:T(8,128)(2,1)S(1)}, bf16[256,384]{1,0:T(8,128)(2,1)S(1)}, u32[]{:S(2)}, u32[]{:S(2)}) %collective-permute-start.6) | collective-permute-done | bytes 196640 | tf_op jit(solution)/shard_map/ppermute | solution.py:36
  162.3 2.4 collective-permute-done.8.rest_2_
  164.7 2.7 collective-permute-start.13
  168.9 4.2 %collective-permute-done.12.rest_6_ = bf16[128,768]{1,0:T(8,128)(2,1)S(1)} collective-permute-done((bf16[128,768]{1,0:T(8,128)(2,1)S(1)}, bf16[128,768]{1,0:T(8,128)(2,1)S(1)}, u32[]{:S(2)}, u32[]{:S(2)}) %collective-permute-start.12) | collective-permute-done | bytes 196640 | tf_op jit(solution)/shard_map/ppermute | solution.py:36
  173.2 7.2 %attention.5 = (bf16[256,384]{1,0:T(8,128)(2,1)S(1)}, bf16[128,3072]{1,0:T(8,128)(2,1)S(1)}) custom-call(s32[13]{0:T(128)S(1)} %stack.165.meta, bf16[128,768]{1,0:T(8,128)(2,1)S(1)} %get-tuple-element.23.rest_0_.hidden0, bf16[128,768]{1,0:T(8,128)(2,1)S(1)} %get-tuple-element.24.rest_1_.hidden1, bf16[128,768]{1,0:T(8,128)(2,1)S(1)} %collective-permute-done.8.rest_2_, ...), custom_call_target="tpu_custom_call" | custom-call | flops 1811939328 | bytes 10000000 | tf_op jit(solution)/shard_map/attention/pallas_call | solution.py:196
  180.8 2.9 %collective-permute-start.15 = (bf16[256,384]{1,0:T(8,128)(2,1)S(1)}, bf16[256,384]{1,0:T(8,128)(2,1)S(1)}, u32[]{:S(2)}, u32[]{:S(2)}) collective-permute-start(bf16[256,384]{1,0:T(8,128)(2,1)S(1)} %get-tuple-element.25.a0), channel_id=1, source_target_pairs={{0,16},{32,48},{64,80},{96,112},{16,0},{48,32},{80,64},{112,96},{1... | collective-permute-start | bytes 589832 | tf_op jit(solution)/shard_map/ppermute | solution.py:36
  185.4 1.9 fetch.4.w
  187.3 2.5 collective-permute-done.15.a2
  192.2 3.4 %collective-permute-start.17 = (bf16[128,768]{1,0:T(8,128)(2,1)S(1)}, bf16[128,768]{1,0:T(8,128)(2,1)S(1)}, u32[]{:S(2)}, u32[]{:S(2)}) collective-permute-start(bf16[128,768]{1,0:T(8,128)(2,1)S(1)} %get-tuple-element.27.rest_0_.hidden0), channel_id=1, source_target_pairs={{0,64},{32,96},{64,16},{96,48},{16,80},{48,112},{80,0},{112,32},{1... | collective-permute-start | bytes 589832 | tf_op jit(solution)/shard_map/ppermute | solution.py:36
  202.0 8.2 %all-gather.9.cloned.1.call-done = bf16[64,336,384]{2,1,0:T(8,128)(2,1)} async-done(((bf16[2,336,384]{2,1,0:T(8,128)(2,1)}), bf16[64,336,384]{2,1,0:T(8,128)(2,1)}) %all-gather.9.cloned.1.call-update) | async-done | bytes 16515088 | tf_op jit(solution)/shard_map/all_gather | solution.py:326
  210.3 7.2 %attention.6 = (bf16[256,384]{1,0:T(8,128)(2,1)S(1)}, bf16[128,3072]{1,0:T(8,128)(2,1)S(1)}) custom-call(s32[13]{0:T(128)S(1)} %stack.165.meta, bf16[128,768]{1,0:T(8,128)(2,1)S(1)} %get-tuple-element.27.rest_0_.hidden0, bf16[128,768]{1,0:T(8,128)(2,1)S(1)} %get-tuple-element.28.rest_1_.hidden1, bf16[128,768]{1,0:T(8,128)(2,1)S(1)} %collective-permute-done.17.rest_2_, ...), custom_call_target="tpu_custom_call" | custom-call | flops 1811939328 | bytes 10000000 | tf_op jit(solution)/shard_map/attention/pallas_call | solution.py:196
  218.8 2.6 collective-permute-start.24
  224.2 5.0 %collective-permute-done.24.a2 = bf16[256,384]{1,0:T(8,128)(2,1)S(1)} collective-permute-done((bf16[256,384]{1,0:T(8,128)(2,1)S(1)}, bf16[256,384]{1,0:T(8,128)(2,1)S(1)}, u32[]{:S(2)}, u32[]{:S(2)}) %collective-permute-start.24) | collective-permute-done | bytes 196640 | tf_op jit(solution)/shard_map/ppermute | solution.py:36
  230.8 2.0 collective-permute-start.26
  234.3 2.7 collective-permute-start.28
  238.0 2.3 collective-permute-start.31
  240.2 2.1 collective-permute-done.27.rest_3_
  242.4 3.3 %collective-permute-done.30.rest_6_ = bf16[128,768]{1,0:T(8,128)(2,1)S(1)} collective-permute-done((bf16[128,768]{1,0:T(8,128)(2,1)S(1)}, bf16[128,768]{1,0:T(8,128)(2,1)S(1)}, u32[]{:S(2)}, u32[]{:S(2)}) %collective-permute-start.30) | collective-permute-done | bytes 196640 | tf_op jit(solution)/shard_map/ppermute | solution.py:36
  246.9 7.7 %attention.7 = (bf16[128,384]{1,0:T(8,128)(2,1)S(1)}, bf16[128,384]{1,0:T(8,128)(2,1)}) custom-call(s32[13]{0:T(128)S(1)} %copy-done.3, bf16[128,768]{1,0:T(8,128)(2,1)S(1)} %get-tuple-element.31.rest_0_, bf16[128,768]{1,0:T(8,128)(2,1)S(1)} %get-tuple-element.32.rest_1_, bf16[128,768]{1,0:T(8,128)(2,1)S(1)} %collective-permute-done.26.rest_2_, ...), custom_call_target="tpu_custom_call" | custom-call | flops 1811939328 | bytes 10000000 | tf_op jit(solution)/shard_map/attention/pallas_call | solution.py:196
  255.9 4.9 %collective-permute-start.33 = (bf16[128,384]{1,0:T(8,128)(2,1)}, bf16[128,384]{1,0:T(8,128)(2,1)S(1)}, u32[]{:S(2)}, u32[]{:S(2)}) collective-permute-start(bf16[128,384]{1,0:T(8,128)(2,1)} %get-tuple-element.34), channel_id=1, source_target_pairs={{0,16},{32,48},{16,0},{48,32},{1,17},{33,49},{17,1},{49,33},{2,18}... | collective-permute-start | bytes 294920 | tf_op jit(solution)/shard_map/ppermute | solution.py:36
  262.9 4.6 %all-gather.11.cloned.1.call-done = bf16[64,192,384]{2,1,0:T(8,128)(2,1)} async-done(((bf16[2,192,384]{2,1,0:T(8,128)(2,1)}), bf16[64,192,384]{2,1,0:T(8,128)(2,1)}) %all-gather.11.cloned.1.call-update) | async-done | bytes 9437200 | tf_op jit(solution)/shard_map/all_gather | solution.py:328
  268.1 5.3 %finish.1 = (bf16[128,3072]{1,0:T(8,128)(2,1)S(1)}, bf16[128,3072]{1,0:T(8,128)(2,1)S(1)}) custom-call(s32[13]{0:T(128)S(1)} %copy-done.4, bf16[128,384]{1,0:T(8,128)(2,1)S(1)} %get-tuple-element.33.a0, bf16[128,384]{1,0:T(8,128)(2,1)S(1)} %collective-permute-done.32.a1, bf16[128,384]{1,0:T(8,128)(2,1)S(1)} %collective-permute-done.33.a2, ...), custom_call_target="tpu_custom_call" | custom-call | flops 1207959552 | bytes 13000000 | tf_op jit(solution)/shard_map/finish/pallas_call | solution.py:228
  273.5 2.2 collective-permute-start.38
  275.6 1.9 collective-permute-done.38
  (136 shorter events, 59.7 us)
Async XLA Ops:
  6.5 130.1 %all-gather.7.cloned.1.call-start = ((), (), s32[]{:S(2)}) async-start(), calls=%async_computation.2 | async-start | bytes 19464192 | tf_op jit(solution)/shard_map/all_gather | solution.py:325
  62.5 147.8 %all-gather.9.cloned.1.call-start = ((), (), s32[]{:S(2)}) async-start(), calls=%async_computation.3 | async-start | bytes 17031168 | tf_op jit(solution)/shard_map/all_gather | solution.py:326
  63.5 203.9 %all-gather.11.cloned.1.call-start = ((), (), s32[]{:S(2)}) async-start(), calls=%async_computation.4 | async-start | bytes 9732096 | tf_op jit(solution)/shard_map/all_gather | solution.py:328
  73.9 28.4 %collective-permute-start.4 = (bf16[128,3072]{1,0:T(8,128)(2,1)}, bf16[128,3072]{1,0:T(8,128)(2,1)}, u32[]{:S(2)}, u32[]{:S(2)}) collective-permute-start(bf16[128,3072]{1,0:T(8,128)(2,1)} %dynamic-slice_bitcast_fusion), channel_id=1, source_target_pairs={{0,80},{32,112},{64,16},{96,48},{16,64},{48,96},{80,0},{112,32},{1... | collective-permute-start | bytes 2359304 | tf_op jit(solution)/shard_map/ppermute | solution.py:36
  76.3 22.5 %collective-permute-start.1 = (f32[2,4,3072]{2,1,0:T(4,128)S(1)}, f32[2,4,3072]{2,1,0:T(4,128)S(1)}, u32[]{:S(2)}, u32[]{:S(2)}) collective-permute-start(f32[2,4,3072]{2,1,0:T(4,128)S(1)} %maximum_select_fusion.1), channel_id=1, source_target_pairs={{0,64},{32,96},{64,16},{96,48},{16,80},{48,112},{80,0},{112,32},{1... | collective-permute-start | bytes 294920 | tf_op jit(solution)/shard_map/ppermute | solution.py:36
  76.4 22.5 %collective-permute-start.2 = (f32[2,4,3072]{2,1,0:T(4,128)S(1)}, f32[2,4,3072]{2,1,0:T(4,128)S(1)}, u32[]{:S(2)}, u32[]{:S(2)}) collective-permute-start(f32[2,4,3072]{2,1,0:T(4,128)S(1)} %maximum_select_fusion.1), channel_id=1, source_target_pairs={{0,16},{32,48},{64,80},{96,112},{16,0},{48,32},{80,64},{112,96},{1... | collective-permute-start | bytes 294920 | tf_op jit(solution)/shard_map/ppermute | solution.py:36
  77.9 21.0 %collective-permute-start.3 = (f32[2,4,3072]{2,1,0:T(4,128)S(1)}, f32[2,4,3072]{2,1,0:T(4,128)S(1)}, u32[]{:S(2)}, u32[]{:S(2)}) collective-permute-start(f32[2,4,3072]{2,1,0:T(4,128)S(1)} %maximum_select_fusion.1), channel_id=1, source_target_pairs={{0,80},{32,112},{64,0},{96,32},{16,64},{48,96},{80,16},{112,48},{1... | collective-permute-start | bytes 294920 | tf_op jit(solution)/shard_map/ppermute | solution.py:36
  143.5 7.5 %collective-permute-start.5 = (bf16[256,384]{1,0:T(8,128)(2,1)S(1)}, bf16[256,384]{1,0:T(8,128)(2,1)S(1)}, u32[]{:S(2)}, u32[]{:S(2)}) collective-permute-start(bf16[256,384]{1,0:T(8,128)(2,1)S(1)} %attention.4.a0), channel_id=1, source_target_pairs={{0,64},{32,96},{64,16},{96,48},{16,80},{48,112},{80,0},{112,32},{1... | collective-permute-start | bytes 589832 | tf_op jit(solution)/shard_map/ppermute | solution.py:36
  144.9 11.6 %collective-permute-start.6 = (bf16[256,384]{1,0:T(8,128)(2,1)S(1)}, bf16[256,384]{1,0:T(8,128)(2,1)S(1)}, u32[]{:S(2)}, u32[]{:S(2)}) collective-permute-start(bf16[256,384]{1,0:T(8,128)(2,1)S(1)} %attention.4.a0), channel_id=1, source_target_pairs={{0,16},{32,48},{64,80},{96,112},{16,0},{48,32},{80,64},{112,96},{1... | collective-permute-start | bytes 589832 | tf_op jit(solution)/shard_map/ppermute | solution.py:36
  147.5 9.0 %collective-permute-start.7 = (bf16[256,384]{1,0:T(8,128)(2,1)S(1)}, bf16[256,384]{1,0:T(8,128)(2,1)S(1)}, u32[]{:S(2)}, u32[]{:S(2)}) collective-permute-start(bf16[256,384]{1,0:T(8,128)(2,1)S(1)} %attention.4.a0), channel_id=1, source_target_pairs={{0,80},{32,112},{64,0},{96,32},{16,64},{48,96},{80,16},{112,48},{1... | collective-permute-start | bytes 589832 | tf_op jit(solution)/shard_map/ppermute | solution.py:36
  158.1 6.6 %collective-permute-start.8 = (bf16[128,768]{1,0:T(8,128)(2,1)S(1)}, bf16[128,768]{1,0:T(8,128)(2,1)S(1)}, u32[]{:S(2)}, u32[]{:S(2)}) collective-permute-start(bf16[128,768]{1,0:T(8,128)(2,1)S(1)} %get-tuple-element.23.rest_0_.hidden0), channel_id=1, source_target_pairs={{0,64},{32,96},{64,16},{96,48},{16,80},{48,112},{80,0},{112,32},{1... | collective-permute-start | bytes 589832 | tf_op jit(solution)/shard_map/ppermute | solution.py:36
  160.8 7.4 %collective-permute-start.10 = (bf16[128,768]{1,0:T(8,128)(2,1)S(1)}, bf16[128,768]{1,0:T(8,128)(2,1)S(1)}, u32[]{:S(2)}, u32[]{:S(2)}) collective-permute-start(bf16[128,768]{1,0:T(8,128)(2,1)S(1)} %get-tuple-element.23.rest_0_.hidden0), channel_id=1, source_target_pairs={{0,80},{32,112},{64,0},{96,32},{16,64},{48,96},{80,16},{112,48},{1... | collective-permute-start | bytes 589832 | tf_op jit(solution)/shard_map/ppermute | solution.py:36
  162.2 6.8 %collective-permute-start.9 = (bf16[128,768]{1,0:T(8,128)(2,1)S(1)}, bf16[128,768]{1,0:T(8,128)(2,1)S(1)}, u32[]{:S(2)}, u32[]{:S(2)}) collective-permute-start(bf16[128,768]{1,0:T(8,128)(2,1)S(1)} %get-tuple-element.24.rest_1_.hidden1), channel_id=1, source_target_pairs={{0,64},{32,96},{64,16},{96,48},{16,80},{48,112},{80,0},{112,32},{1... | collective-permute-start | bytes 589832 | tf_op jit(solution)/shard_map/ppermute | solution.py:36
  164.7 8.5 %collective-permute-start.12 = (bf16[128,768]{1,0:T(8,128)(2,1)S(1)}, bf16[128,768]{1,0:T(8,128)(2,1)S(1)}, u32[]{:S(2)}, u32[]{:S(2)}) collective-permute-start(bf16[128,768]{1,0:T(8,128)(2,1)S(1)} %collective-permute-done.8.rest_2_), channel_id=1, source_target_pairs={{0,64},{32,96},{64,16},{96,48},{16,80},{48,112},{80,0},{112,32},{1... | collective-permute-start | bytes 589832 | tf_op jit(solution)/shard_map/ppermute | solution.py:36
  164.7 8.4 %collective-permute-start.13 = (bf16[128,768]{1,0:T(8,128)(2,1)S(1)}, bf16[128,768]{1,0:T(8,128)(2,1)S(1)}, u32[]{:S(2)}, u32[]{:S(2)}) collective-permute-start(bf16[128,768]{1,0:T(8,128)(2,1)S(1)} %collective-permute-done.11.rest_5_), channel_id=1, source_target_pairs={{0,80},{32,112},{64,0},{96,32},{16,64},{48,96},{80,16},{112,48},{1... | collective-permute-start | bytes 589832 | tf_op jit(solution)/shard_map/ppermute | solution.py:36
  180.3 7.0 %collective-permute-start.14 = (bf16[256,384]{1,0:T(8,128)(2,1)S(1)}, bf16[256,384]{1,0:T(8,128)(2,1)S(1)}, u32[]{:S(2)}, u32[]{:S(2)}) collective-permute-start(bf16[256,384]{1,0:T(8,128)(2,1)S(1)} %get-tuple-element.25.a0), channel_id=1, source_target_pairs={{0,64},{32,96},{64,16},{96,48},{16,80},{48,112},{80,0},{112,32},{1... | collective-permute-start | bytes 589832 | tf_op jit(solution)/shard_map/ppermute | solution.py:36
  180.8 9.0 %collective-permute-start.15 = (bf16[256,384]{1,0:T(8,128)(2,1)S(1)}, bf16[256,384]{1,0:T(8,128)(2,1)S(1)}, u32[]{:S(2)}, u32[]{:S(2)}) collective-permute-start(bf16[256,384]{1,0:T(8,128)(2,1)S(1)} %get-tuple-element.25.a0), channel_id=1, source_target_pairs={{0,16},{32,48},{64,80},{96,112},{16,0},{48,32},{80,64},{112,96},{1... | collective-permute-start | bytes 589832 | tf_op jit(solution)/shard_map/ppermute | solution.py:36
  183.7 6.9 %collective-permute-start.16 = (bf16[256,384]{1,0:T(8,128)(2,1)S(1)}, bf16[256,384]{1,0:T(8,128)(2,1)S(1)}, u32[]{:S(2)}, u32[]{:S(2)}) collective-permute-start(bf16[256,384]{1,0:T(8,128)(2,1)S(1)} %get-tuple-element.25.a0), channel_id=1, source_target_pairs={{0,80},{32,112},{64,0},{96,32},{16,64},{48,96},{80,16},{112,48},{1... | collective-permute-start | bytes 589832 | tf_op jit(solution)/shard_map/ppermute | solution.py:36
  192.2 7.1 %collective-permute-start.17 = (bf16[128,768]{1,0:T(8,128)(2,1)S(1)}, bf16[128,768]{1,0:T(8,128)(2,1)S(1)}, u32[]{:S(2)}, u32[]{:S(2)}) collective-permute-start(bf16[128,768]{1,0:T(8,128)(2,1)S(1)} %get-tuple-element.27.rest_0_.hidden0), channel_id=1, source_target_pairs={{0,64},{32,96},{64,16},{96,48},{16,80},{48,112},{80,0},{112,32},{1... | collective-permute-start | bytes 589832 | tf_op jit(solution)/shard_map/ppermute | solution.py:36
  195.9 14.4 %collective-permute-start.18 = (bf16[128,768]{1,0:T(8,128)(2,1)S(1)}, bf16[128,768]{1,0:T(8,128)(2,1)S(1)}, u32[]{:S(2)}, u32[]{:S(2)}) collective-permute-start(bf16[128,768]{1,0:T(8,128)(2,1)S(1)} %get-tuple-element.28.rest_1_.hidden1), channel_id=1, source_target_pairs={{0,64},{32,96},{64,16},{96,48},{16,80},{48,112},{80,0},{112,32},{1... | collective-permute-start | bytes 589832 | tf_op jit(solution)/shard_map/ppermute | solution.py:36
  197.0 13.3 %collective-permute-start.19 = (bf16[128,768]{1,0:T(8,128)(2,1)S(1)}, bf16[128,768]{1,0:T(8,128)(2,1)S(1)}, u32[]{:S(2)}, u32[]{:S(2)}) collective-permute-start(bf16[128,768]{1,0:T(8,128)(2,1)S(1)} %get-tuple-element.27.rest_0_.hidden0), channel_id=1, source_target_pairs={{0,80},{32,112},{64,0},{96,32},{16,64},{48,96},{80,16},{112,48},{1... | collective-permute-start | bytes 589832 | tf_op jit(solution)/shard_map/ppermute | solution.py:36
  199.3 11.0 %collective-permute-start.21 = (bf16[128,768]{1,0:T(8,128)(2,1)S(1)}, bf16[128,768]{1,0:T(8,128)(2,1)S(1)}, u32[]{:S(2)}, u32[]{:S(2)}) collective-permute-start(bf16[128,768]{1,0:T(8,128)(2,1)S(1)} %collective-permute-done.17.rest_2_), channel_id=1, source_target_pairs={{0,64},{32,96},{64,16},{96,48},{16,80},{48,112},{80,0},{112,32},{1... | collective-permute-start | bytes 589832 | tf_op jit(solution)/shard_map/ppermute | solution.py:36
  200.7 9.6 %collective-permute-start.22 = (bf16[128,768]{1,0:T(8,128)(2,1)S(1)}, bf16[128,768]{1,0:T(8,128)(2,1)S(1)}, u32[]{:S(2)}, u32[]{:S(2)}) collective-permute-start(bf16[128,768]{1,0:T(8,128)(2,1)S(1)} %collective-permute-done.20.rest_5_), channel_id=1, source_target_pairs={{0,80},{32,112},{64,0},{96,32},{16,64},{48,96},{80,16},{112,48},{1... | collective-permute-start | bytes 589832 | tf_op jit(solution)/shard_map/ppermute | solution.py:36
  217.5 6.7 %collective-permute-start.23 = (bf16[256,384]{1,0:T(8,128)(2,1)S(1)}, bf16[256,384]{1,0:T(8,128)(2,1)S(1)}, u32[]{:S(2)}, u32[]{:S(2)}) collective-permute-start(bf16[256,384]{1,0:T(8,128)(2,1)S(1)} %get-tuple-element.29.a0), channel_id=1, source_target_pairs={{0,64},{32,96},{64,16},{96,48},{16,80},{48,112},{80,0},{112,32},{1... | collective-permute-start | bytes 589832 | tf_op jit(solution)/shard_map/ppermute | solution.py:36
  218.8 10.4 %collective-permute-start.24 = (bf16[256,384]{1,0:T(8,128)(2,1)S(1)}, bf16[256,384]{1,0:T(8,128)(2,1)S(1)}, u32[]{:S(2)}, u32[]{:S(2)}) collective-permute-start(bf16[256,384]{1,0:T(8,128)(2,1)S(1)} %get-tuple-element.29.a0), channel_id=1, source_target_pairs={{0,16},{32,48},{64,80},{96,112},{16,0},{48,32},{80,64},{112,96},{1... | collective-permute-start | bytes 589832 | tf_op jit(solution)/shard_map/ppermute | solution.py:36
  221.4 7.8 %collective-permute-start.25 = (bf16[256,384]{1,0:T(8,128)(2,1)S(1)}, bf16[256,384]{1,0:T(8,128)(2,1)S(1)}, u32[]{:S(2)}, u32[]{:S(2)}) collective-permute-start(bf16[256,384]{1,0:T(8,128)(2,1)S(1)} %get-tuple-element.29.a0), channel_id=1, source_target_pairs={{0,80},{32,112},{64,0},{96,32},{16,64},{48,96},{80,16},{112,48},{1... | collective-permute-start | bytes 589832 | tf_op jit(solution)/shard_map/ppermute | solution.py:36
  234.3 8.1 %collective-permute-start.27 = (bf16[128,768]{1,0:T(8,128)(2,1)S(1)}, bf16[128,768]{1,0:T(8,128)(2,1)S(1)}, u32[]{:S(2)}, u32[]{:S(2)}) collective-permute-start(bf16[128,768]{1,0:T(8,128)(2,1)S(1)} %get-tuple-element.32.rest_1_), channel_id=1, source_target_pairs={{0,64},{32,96},{64,16},{96,48},{16,80},{48,112},{80,0},{112,32},{1... | collective-permute-start | bytes 589832 | tf_op jit(solution)/shard_map/ppermute | solution.py:36
  234.3 8.1 %collective-permute-start.28 = (bf16[128,768]{1,0:T(8,128)(2,1)S(1)}, bf16[128,768]{1,0:T(8,128)(2,1)S(1)}, u32[]{:S(2)}, u32[]{:S(2)}) collective-permute-start(bf16[128,768]{1,0:T(8,128)(2,1)S(1)} %get-tuple-element.31.rest_0_), channel_id=1, source_target_pairs={{0,80},{32,112},{64,0},{96,32},{16,64},{48,96},{80,16},{112,48},{1... | collective-permute-start | bytes 589832 | tf_op jit(solution)/shard_map/ppermute | solution.py:36
  237.3 8.4 %collective-permute-start.30 = (bf16[128,768]{1,0:T(8,128)(2,1)S(1)}, bf16[128,768]{1,0:T(8,128)(2,1)S(1)}, u32[]{:S(2)}, u32[]{:S(2)}) collective-permute-start(bf16[128,768]{1,0:T(8,128)(2,1)S(1)} %collective-permute-done.26.rest_2_), channel_id=1, source_target_pairs={{0,64},{32,96},{64,16},{96,48},{16,80},{48,112},{80,0},{112,32},{1... | collective-permute-start | bytes 589832 | tf_op jit(solution)/shard_map/ppermute | solution.py:36
  238.0 8.2 %collective-permute-start.31 = (bf16[128,768]{1,0:T(8,128)(2,1)S(1)}, bf16[128,768]{1,0:T(8,128)(2,1)S(1)}, u32[]{:S(2)}, u32[]{:S(2)}) collective-permute-start(bf16[128,768]{1,0:T(8,128)(2,1)S(1)} %collective-permute-done.29.rest_5_), channel_id=1, source_target_pairs={{0,80},{32,112},{64,0},{96,32},{16,64},{48,96},{80,16},{112,48},{1... | collective-permute-start | bytes 589832 | tf_op jit(solution)/shard_map/ppermute | solution.py:36
  254.6 12.8 %collective-permute-start.32 = (bf16[128,384]{1,0:T(8,128)(2,1)}, bf16[128,384]{1,0:T(8,128)(2,1)S(1)}, u32[]{:S(2)}, u32[]{:S(2)}) collective-permute-start(bf16[128,384]{1,0:T(8,128)(2,1)} %get-tuple-element.34), channel_id=1, source_target_pairs={{64,16},{96,48},{80,0},{112,32},{65,17},{97,49},{81,1},{113,33},{6... | collective-permute-start | bytes 294920 | tf_op jit(solution)/shard_map/ppermute | solution.py:36
  255.9 11.5 %collective-permute-start.33 = (bf16[128,384]{1,0:T(8,128)(2,1)}, bf16[128,384]{1,0:T(8,128)(2,1)S(1)}, u32[]{:S(2)}, u32[]{:S(2)}) collective-permute-start(bf16[128,384]{1,0:T(8,128)(2,1)} %get-tuple-element.34), channel_id=1, source_target_pairs={{0,16},{32,48},{16,0},{48,32},{1,17},{33,49},{17,1},{49,33},{2,18}... | collective-permute-start | bytes 294920 | tf_op jit(solution)/shard_map/ppermute | solution.py:36
  (21 other events, 158.0 us)
Sparse Core Ops, SparseCore 0:
  62.6 74.0 all-gather.6
  139.0 71.2 all-gather.8
  212.6 54.8 all-gather.10
where the time goes:
time: 290 us; the launch traced here: 286 us
  waiting for transfers between devices  100 us (34%)
  starting transfers between devices  59.9 us (21%)
  blocking collectives  51.4 us (18%)
  Pallas kernels  45.9 us (16%)
  between operations  14 us (5%)
  local copies, waits for them, and re-layouts  7.61 us (3%)
  other arithmetic  6.91 us (2%)
    ppermute x37, starting transfers between devices, device_permute(): return lax.ppermute(value, ('z_lo', 'core', 'z_hi'), pairs)  56.1 us
    ppermute x37, waiting for transfers between devices, device_permute(): return lax.ppermute(value, ('z_lo', 'core', 'z_hi'), pairs)  52.3 us
    all_gather x1, waiting for transfers between devices, on_device(): lax.all_gather(jnp.concatenate([shards[0], shards[1]], axis=1), plane)  33 us
    all_to_all x1, blocking collectives, weight_shards(): mixed = lax.all_to_all(packed, ('z_hi', 'x', 'y'), 0, 0)  30.4 us
    pallas_call x4, Pallas kernels, attention(): pl.pallas_call(functools.partial(attention_kernel, first, keeps, last), o...  29 us
    all_to_all x1, blocking collectives, weight_shards(): shards = lax.all_to_all(blocks, ('z_lo', 'core', 'z_hi'), 0, 0)  21 us
    all_gather x1, waiting for transfers between devices, on_device(): lax.all_gather(jnp.concatenate([shards[2], shards[3, :, :144]], axis=1),...  8.23 us
  transfers between devices with their start and end apart: 42, of which 22 were waited for; matrix products, arithmetic and copies ran while one was open for 3% of the time, Pallas kernels for 14%

commit v1 on v0

--- a/solution.py
+++ b/solution.py
@@ -21,7 +21,6 @@
 AXES = ("z_lo", "core", "z_hi", "x", "y")
 VMEM_LIMIT = 48 * 1024 * 1024
 HBM = pl.BlockSpec(memory_space=pl.ANY)
-SMEM = pl.BlockSpec(memory_space=pltpu.SMEM)
 VMEM = pl.BlockSpec(memory_space=pltpu.VMEM)
 
 
@@ -59,16 +58,26 @@
     return (values * cosine + partner * sine).astype(jnp.bfloat16)
 
 
-def attention_kernel(first, keeps, last, meta, *rest):
-    states, (mods, cosine, sine, weights), outs, (w, y, both, sems, keep_sem) = rest[:8], rest[8:12], rest[12:-5], rest[-5:]
+def places():
+    z_lo, core, z_hi = (lax.axis_index(a) for a in ("z_lo", "core", "z_hi"))
+    z = 2 * z_hi + z_lo
+    around = [lax.rem(z + k, 4) for k in (0, 3, 2, 1)]
+    return z_lo, core, z_hi, around, [around[0], around[1], around[3], around[2]]
+
+
+def attention_kernel(first, keeps, last, *rest):
+    _, _, z_hi, _, order = places()
+    if not (keeps or last):
+        order = [0, 1, 2, 3]
+    states, (mods, tables, weights), outs, (w, y, both, sems, keep_sem) = rest[:8], rest[8:11], rest[11:-5], rest[-5:]
     if keeps:
         kept = outs[-1]
         for b in range(2):
 
-            @pl.when(meta[6] == b)
+            @pl.when(z_hi == b)
             def keep(pieces=states[b::2]):
                 for k, p in enumerate(pieces):
-                    place = pl.ds(pl.multiple_of(meta[k] * QD, QD), QD)
+                    place = pl.ds(pl.multiple_of(order[k] * QD, QD), QD)
                     pltpu.make_async_copy(p, kept.at[:, place], keep_sem).start()
 
     for i in range(4):
@@ -88,7 +97,7 @@
             total += jnp.sum((p[...].astype(jnp.float32) - center) ** 2, axis=1, keepdims=True)
         inverse = 1.0 / jnp.sqrt(total / D + 1e-06)
         for k, p in enumerate(pieces):
-            q = meta[k]
+            q = order[k]
             normed = (p[...].astype(jnp.float32) - center) * inverse
             shift = mods[q, b, 0:1, :]
             scale = mods[q, b, 1:2, :]
@@ -102,9 +111,8 @@
     lane = lax.broadcasted_iota(jnp.int32, (TOK, HSZ), 1)
     first = (lane % 64) < 32
     for b in range(2):
-        live = lane < meta[4 + b]
         lo = b * TOK
-        cb, sb = cosine[lo : lo + TOK, :], sine[lo : lo + TOK, :]
+        cb, sb, live = tables[0, lo : lo + TOK, :], tables[1, lo : lo + TOK, :], tables[2, lo : lo + TOK, :] > 0.0
         for h in range(3):
             query = rotate(qkv[lo : lo + TOK, h * HSZ : (h + 1) * HSZ].astype(jnp.float32), cb, sb, first)
             key = rotate(qkv[lo : lo + TOK, QH + h * HSZ : QH + (h + 1) * HSZ].astype(jnp.float32), cb, sb, first)
@@ -121,8 +129,8 @@
             else:
                 outs[0][lo : lo + TOK, cols] = mixed
     if last:
-        outs[0][...] = both[meta[6]]
-        outs[1][...] = both[1 - meta[6]]
+        outs[0][...] = both[z_hi]
+        outs[1][...] = both[1 - z_hi]
     if keeps:
         pltpu.make_async_copy(kept, kept, keep_sem).wait()
 
@@ -147,9 +155,10 @@
     )(weights)
 
 
-def project_kernel(meta, a0, a1, a2, a3, hidden0, hidden1, gate, w, out0, out1, a):
+def project_kernel(a0, a1, a2, a3, hidden0, hidden1, gate, w, out0, out1, a):
+    z_lo, core, b, around, order = places()
     for k, part in enumerate((a0, a1, a2, a3)):
-        a[:, pl.ds(pl.multiple_of(meta[7 + k] * QH, QH), QH)] = part[...]
+        a[:, pl.ds(pl.multiple_of(around[k] * QH, QH), QH)] = part[...]
     for n in range(2):
         cols = pl.ds(n * QH, QH)
         proj = jnp.dot(a[...], w[n].reshape(HD, QH), preferred_element_type=jnp.float32).astype(jnp.bfloat16)
@@ -158,37 +167,37 @@
             out[:, cols] = (hidden[:, cols].astype(jnp.float32) + change).astype(jnp.bfloat16)
 
 
-def finish_kernel(meta, a0, a1, a2, a3, *rest):
+def finish_kernel(a0, a1, a2, a3, *rest):
     states, (gate, weights, kept1, kept2, stay, leave, w, a, early, sems) = rest[:8], rest[8:]
     copies = []
     for k, ring in enumerate((0, 1, 3, 2)):
         copies.append(pltpu.make_async_copy(weights.at[:, :, :, pl.ds(ring * 48, 48), :], w.at[k], sems.at[k]))
         copies[-1].start()
-    for z_lo, kept in enumerate((kept1, kept2)):
-
-        @pl.when(meta[11] == z_lo)
+    for i, kept in enumerate((kept1, kept2)):
+
+        @pl.when(lax.axis_index("z_lo") == i)
         def bring(kept=kept):
             pltpu.make_async_copy(kept, early, sems.at[4]).start()
 
+    z_lo, core, b, around, order = places()
     for k, part in enumerate((a0, a1, a2, a3)):
-        a[:, pl.ds(pl.multiple_of(meta[7 + k] * QH, QH), QH)] = part[...]
+        a[:, pl.ds(pl.multiple_of(around[k] * QH, QH), QH)] = part[...]
     pltpu.make_async_copy(kept1, early, sems.at[4]).wait()
-    b = meta[6]
     for k in range(4):
         copies[k].wait()
-        q = meta[k]
+        q = order[k]
         for n in range(2):
             cols = pl.ds(n * QH, QH)
             proj = jnp.dot(a[...], w[k, n].reshape(HD, QH), preferred_element_type=jnp.float32).astype(jnp.bfloat16)
             hidden = jnp.where(b == 0, states[2 * k][:, cols], states[2 * k + 1][:, cols])
             change = gate[q, pl.ds(b, 1), cols] * proj.astype(jnp.float32)
             place = pl.ds(pl.multiple_of(q * QD + n * QH, QH), QH)
-            late = jnp.where(meta[11] == 0, (hidden.astype(jnp.float32) + change).astype(jnp.bfloat16), hidden)
-            stay[:, place] = jnp.where(meta[11] == meta[12], late, early[:, place])
-            leave[:, place] = jnp.where(meta[11] == meta[12], early[:, place], late)
-
-
-def attention(meta, pieces, mods, cosine, sine, weights, first, keeps, last):
+            late = jnp.where(z_lo == 0, (hidden.astype(jnp.float32) + change).astype(jnp.bfloat16), hidden)
+            stay[:, place] = jnp.where(z_lo == core, late, early[:, place])
+            leave[:, place] = jnp.where(z_lo == core, early[:, place], late)
+
+
+def attention(pieces, mods, tables, weights, first, keeps, last):
     if last:
         attended = (jax.ShapeDtypeStruct((TOK, QH), jnp.bfloat16),) * 2
     else:
@@ -196,7 +205,7 @@
     return pl.pallas_call(
         functools.partial(attention_kernel, first, keeps, last),
         out_shape=attended + (jax.ShapeDtypeStruct((TOK, D), jnp.bfloat16),) * keeps,
-        in_specs=[SMEM] + [VMEM] * 11 + [HBM],
+        in_specs=[VMEM] * 10 + [HBM],
         out_specs=(VMEM,) * len(attended) + (HBM,) * keeps,
         scratch_shapes=[
             pltpu.VMEM((4, 8, 2, 48, 3 * QH), jnp.bfloat16),
@@ -208,27 +217,27 @@
         compiler_params=pltpu.CompilerParams(vmem_limit_bytes=VMEM_LIMIT),
         cost_estimate=pl.CostEstimate(flops=2 * ROWS * D * 3 * QH, bytes_accessed=10000000, transcendentals=100000),
         name="attention",
-    )(meta, *pieces, mods, cosine, sine, weights)
-
-
-def project(meta, parts, hidden, gate, weights):
+    )(*pieces, mods, tables, weights)
+
+
+def project(parts, hidden, gate, weights):
     return pl.pallas_call(
         project_kernel,
         out_shape=(jax.ShapeDtypeStruct((TOK, QD), jnp.bfloat16),) * 2,
-        in_specs=[SMEM] + [VMEM] * 8,
+        in_specs=[VMEM] * 8,
         out_specs=(VMEM, VMEM),
         scratch_shapes=[pltpu.VMEM((ROWS, HD), jnp.bfloat16)],
         compiler_params=pltpu.CompilerParams(vmem_limit_bytes=VMEM_LIMIT),
         cost_estimate=pl.CostEstimate(flops=2 * ROWS * HD * QD, bytes_accessed=4000000, transcendentals=0),
         name="project",
-    )(meta, *parts, *hidden, gate, weights)
-
-
-def finish(meta, parts, pieces, gate, weights, kept):
+    )(*parts, *hidden, gate, weights)
+
+
+def finish(parts, pieces, gate, weights, kept):
     return pl.pallas_call(
         finish_kernel,
         out_shape=(jax.ShapeDtypeStruct((TOK, D), jnp.bfloat16),) * 2,
-        in_specs=[SMEM] + [VMEM] * 13 + [HBM] * 3,
+        in_specs=[VMEM] * 13 + [HBM] * 3,
         out_specs=(VMEM, VMEM),
         scratch_shapes=[
             pltpu.VMEM((4, 2, 16, 2, 48, QH), jnp.bfloat16),
@@ -239,7 +248,7 @@
         compiler_params=pltpu.CompilerParams(vmem_limit_bytes=VMEM_LIMIT),
         cost_estimate=pl.CostEstimate(flops=2 * TOK * HD * D, bytes_accessed=13000000, transcendentals=0),
         name="finish",
-    )(meta, *parts, *pieces, gate, weights, *kept)
+    )(*parts, *pieces, gate, weights, *kept)
 
 
 def pick(options, index):
@@ -311,8 +320,9 @@
     row_angle = (patch // GRID).astype(jnp.float32)[:, None] * frequency
     col_angle = (patch % GRID).astype(jnp.float32)[:, None] * frequency
     angle = jnp.concatenate([row_angle, row_angle, col_angle, col_angle], axis=1)
-    cosine = jnp.cos(angle)
     sine = jnp.sin(angle) * jnp.where(jnp.arange(HSZ) % 64 < 32, -1.0, 1.0).astype(jnp.float32)
+    live = jnp.arange(TOK, dtype=jnp.int32) < jnp.repeat(count, TOK)[:, None]
+    tables = jnp.stack([jnp.cos(angle), sine, live.astype(jnp.float32)])
 
     own = lax.dynamic_index_in_dim(latents, core, 0, keepdims=False)[0]
     other = device_permute(own, lambda a, c: (3 - a, c))
@@ -329,24 +339,21 @@
     front, middle = front.reshape(2, 16, 2, 384, QH), middle.reshape(2, 16, 2, 336, QH)
     final = final.reshape(2, 16, 2, 192, QH)
     weights = [(front, 0), (front, 192), (middle, 0), (middle, 192)]
-    order = [0, 1, 2, 3]
     kept = []
     for layer in range(LAYERS):
-        meta = jnp.stack([jnp.asarray(v, jnp.int32) for v in order + [count[0], count[1], z_hi] + places + [z_lo, core]])
         gathered, first = weights[layer]
-        att = attention(meta, pieces, mods[layer], cosine, sine, gathered, first, layer in (1, 2), layer == LAYERS - 1)
+        att = attention(pieces, mods[layer], tables, gathered, first, layer in (1, 2), layer == LAYERS - 1)
         if layer in (1, 2):
             *att, keep = att
             kept.append(keep)
         if layer < LAYERS - 1:
-            quarter_of = project(meta, ring_gather(att[0]), quarter_of, gates[layer], fetch(gathered, first + 144, att[0]))
+            quarter_of = project(ring_gather(att[0]), quarter_of, gates[layer], fetch(gathered, first + 144, att[0]))
             pieces = ring_gather_rows(*quarter_of)
-            order = [z, (z + 3) % 4, (z + 1) % 4, (z + 2) % 4]
 
     same, cross = att
     moves = [(cross, {1: 2, 3: 0}), (cross, {0: 2, 2: 0}), (same, {1: 0, 3: 2})]
     parts = [same] + [device_permute(value, lambda a, c: (move[a], c) if a in move else None) for value, move in moves]
-    stay, leave = finish(meta, parts, pieces, last_gate, final, kept)
+    stay, leave = finish(parts, pieces, last_gate, final, kept)
     leave = core_swap(leave)
     first = jnp.where(core == 0, stay, leave)
     second = jnp.where(core == 0, leave, stay)

time: 290 us -> 289 us (level)
  Pallas kernels: 45.9 us -> 41.8 us
  waiting for transfers between devices: 100 us -> 104 us
  transfers between devices with their start and end apart: 42 -> 42, of which waited for: 22 -> 22; matrix products, arithmetic and copies ran while one was open for 3% -> 3% of each run, Pallas kernels for 14% -> 12%
where the time goes in v1:
time: 289 us; the launch traced here: 284 us
  waiting for transfers between devices  104 us (36%)
  starting transfers between devices  58.4 us (20%)
  blocking collectives  51.4 us (18%)
  Pallas kernels  41.8 us (14%)
  between operations  14 us (5%)
  other arithmetic  7.19 us (2%)
  local copies, waits for them, and re-layouts  6.95 us (2%)
    ppermute x37, starting transfers between devices, device_permute(): return lax.ppermute(value, ('z_lo', 'core', 'z_hi'), pairs)  55.6 us
    ppermute x37, waiting for transfers between devices, device_permute(): return lax.ppermute(value, ('z_lo', 'core', 'z_hi'), pairs)  54 us
    all_gather x1, waiting for transfers between devices, on_device(): lax.all_gather(jnp.concatenate([shards[0], shards[1]], axis=1), plane)  32.6 us
    all_to_all x1, blocking collectives, weight_shards(): mixed = lax.all_to_all(packed, ('z_hi', 'x', 'y'), 0, 0)  30.4 us
    pallas_call x4, Pallas kernels, attention(): pl.pallas_call(functools.partial(attention_kernel, first, keeps, last), o...  26.6 us
    all_to_all x1, blocking collectives, weight_shards(): shards = lax.all_to_all(blocks, ('z_lo', 'core', 'z_hi'), 0, 0)  21 us
    all_gather x1, waiting for transfers between devices, on_device(): lax.all_gather(jnp.concatenate([shards[2], shards[3, :, :144]], axis=1),...  10.2 us
  transfers between devices with their start and end apart: 42, of which 22 were waited for; matrix products, arithmetic and copies ran while one was open for 3% of the time, Pallas kernels for 12%

profile of v1, /device:TPU:1, one launch (start us, length us, event | category | flops | bytes accessed | tf_op | source)
XLA Modules:
  0.0 284.0 jit_solution(1899924913465445964)
XLA Ops:
  9.6 30.4 %all_to_all.10.mixed = bf16[32,48,384]{2,1,0:T(8,128)(2,1)S(1)} all-to-all(bf16[32,48,384]{2,1,0:T(8,128)(2,1)S(1)} %pack.1), channel_id=1, replica_groups=mesh['z_lo'=2,'core'=2,'z_hi'=2,'x'=4,'y'=4] {'z_hi','x','y'}, dimensions={0} | all-to-all | bytes 2359296 | tf_op jit(solution)/shard_map/all_to_all | solution.py:285
  40.5 21.0 %all_to_all.11 = bf16[8,192,384]{2,1,0:T(8,128)(2,1)S(1)} all-to-all(bf16[8,192,384]{2,1,0:T(8,128)(2,1)S(1)} %regroup.1), channel_id=1, replica_groups=mesh['z_lo'=2,'core'=2,'z_hi'=2,'x'=4,'y'=4] {'z_lo','core','z_hi'}, dimensions={0} | all-to-all | bytes 2359296 | tf_op jit(solution)/shard_map/all_to_all | solution.py:292
  66.4 2.4 collective-permute-done.35
  73.9 2.3 collective-permute-start
  79.7 19.1 %collective-permute-done.2 = f32[2,4,3072]{2,1,0:T(4,128)S(1)} collective-permute-done((f32[2,4,3072]{2,1,0:T(4,128)S(1)}, f32[2,4,3072]{2,1,0:T(4,128)S(1)}, u32[]{:S(2)}, u32[]{:S(2)}) %collective-permute-start.2) | collective-permute-done | bytes 98336 | tf_op jit(solution)/shard_map/ppermute | solution.py:35
  103.9 32.6 %all-gather.7.cloned.1.call-done = bf16[64,384,384]{2,1,0:T(8,128)(2,1)} async-done(((bf16[2,384,384]{2,1,0:T(8,128)(2,1)}), bf16[64,384,384]{2,1,0:T(8,128)(2,1)}) %all-gather.7.cloned.1.call-update) | async-done | bytes 18874384 | tf_op jit(solution)/shard_map/all_gather | solution.py:335
  136.5 6.3 %attention.4.a0 = bf16[256,384]{1,0:T(8,128)(2,1)S(1)} custom-call(bf16[128,768]{1,0:T(8,128)(2,1)S(1)} %get-tuple-element.79.rest_0_, bf16[128,768]{1,0:T(8,128)(2,1)S(1)} %get-tuple-element.50.rest_1_, bf16[128,768]{1,0:T(8,128)(2,1)S(1)} %get-tuple-element.80.rest_2_, bf16[128,768]{1,0:T(8,128)(2,1)S(1)} %get-tuple-element.49.rest_3_, ...), custom_call_target="tpu_custom_call" | custom-call | flops 1811939328 | bytes 10000000 | tf_op jit(solution)/shard_map/attention/pallas_call | solution.py:205
  144.2 2.6 collective-permute-start.6
  147.9 1.8 fetch.3.w
  150.4 5.4 %collective-permute-done.6.a2 = bf16[256,384]{1,0:T(8,128)(2,1)S(1)} collective-permute-done((bf16[256,384]{1,0:T(8,128)(2,1)S(1)}, bf16[256,384]{1,0:T(8,128)(2,1)S(1)}, u32[]{:S(2)}, u32[]{:S(2)}) %collective-permute-start.6) | collective-permute-done | bytes 196640 | tf_op jit(solution)/shard_map/ppermute | solution.py:35
  157.8 1.8 collective-permute-start.11
  161.1 2.5 collective-permute-done.8.rest_2_
  163.6 2.7 collective-permute-start.13
  167.7 4.2 %collective-permute-done.12.rest_6_ = bf16[128,768]{1,0:T(8,128)(2,1)S(1)} collective-permute-done((bf16[128,768]{1,0:T(8,128)(2,1)S(1)}, bf16[128,768]{1,0:T(8,128)(2,1)S(1)}, u32[]{:S(2)}, u32[]{:S(2)}) %collective-permute-start.12) | collective-permute-done | bytes 196640 | tf_op jit(solution)/shard_map/ppermute | solution.py:35
  171.9 6.6 %attention.5 = (bf16[256,384]{1,0:T(8,128)(2,1)S(1)}, bf16[128,3072]{1,0:T(8,128)(2,1)S(1)}) custom-call(bf16[128,768]{1,0:T(8,128)(2,1)S(1)} %get-tuple-element.23.rest_0_.hidden0, bf16[128,768]{1,0:T(8,128)(2,1)S(1)} %get-tuple-element.24.rest_1_.hidden1, bf16[128,768]{1,0:T(8,128)(2,1)S(1)} %collective-permute-done.8.rest_2_, ...), custom_call_target="tpu_custom_call" | custom-call | flops 1811939328 | bytes 10000000 | tf_op jit(solution)/shard_map/attention/pallas_call | solution.py:205
  179.8 2.6 collective-permute-start.15
  183.6 1.8 fetch.4.w
  185.4 3.7 %collective-permute-done.15.a2 = bf16[256,384]{1,0:T(8,128)(2,1)S(1)} collective-permute-done((bf16[256,384]{1,0:T(8,128)(2,1)S(1)}, bf16[256,384]{1,0:T(8,128)(2,1)S(1)}, u32[]{:S(2)}, u32[]{:S(2)}) %collective-permute-start.15) | collective-permute-done | bytes 196640 | tf_op jit(solution)/shard_map/ppermute | solution.py:35
  190.2 3.2 %collective-permute-start.17 = (bf16[128,768]{1,0:T(8,128)(2,1)S(1)}, bf16[128,768]{1,0:T(8,128)(2,1)S(1)}, u32[]{:S(2)}, u32[]{:S(2)}) collective-permute-start(bf16[128,768]{1,0:T(8,128)(2,1)S(1)} %get-tuple-element.27.rest_0_.hidden0), channel_id=1, source_target_pairs={{0,64},{32,96},{64,16},{96,48},{16,80},{48,112},{80,0},{112,32},{1... | collective-permute-start | bytes 589832 | tf_op jit(solution)/shard_map/ppermute | solution.py:35
  199.9 10.2 %all-gather.9.cloned.1.call-done = bf16[64,336,384]{2,1,0:T(8,128)(2,1)} async-done(((bf16[2,336,384]{2,1,0:T(8,128)(2,1)}), bf16[64,336,384]{2,1,0:T(8,128)(2,1)}) %all-gather.9.cloned.1.call-update) | async-done | bytes 16515088 | tf_op jit(solution)/shard_map/all_gather | solution.py:336
  210.9 6.6 %attention.6 = (bf16[256,384]{1,0:T(8,128)(2,1)S(1)}, bf16[128,3072]{1,0:T(8,128)(2,1)S(1)}) custom-call(bf16[128,768]{1,0:T(8,128)(2,1)S(1)} %get-tuple-element.27.rest_0_.hidden0, bf16[128,768]{1,0:T(8,128)(2,1)S(1)} %get-tuple-element.28.rest_1_.hidden1, bf16[128,768]{1,0:T(8,128)(2,1)S(1)} %collective-permute-done.17.rest_2_, ...), custom_call_target="tpu_custom_call" | custom-call | flops 1811939328 | bytes 10000000 | tf_op jit(solution)/shard_map/attention/pallas_call | solution.py:205
  218.9 2.6 collective-permute-start.24
  225.1 5.4 %collective-permute-done.24.a2 = bf16[256,384]{1,0:T(8,128)(2,1)S(1)} collective-permute-done((bf16[256,384]{1,0:T(8,128)(2,1)S(1)}, bf16[256,384]{1,0:T(8,128)(2,1)S(1)}, u32[]{:S(2)}, u32[]{:S(2)}) %collective-permute-start.24) | collective-permute-done | bytes 196640 | tf_op jit(solution)/shard_map/ppermute | solution.py:35
  232.5 1.8 collective-permute-start.29
  234.3 2.7 collective-permute-start.28
  238.2 2.9 %collective-permute-start.31 = (bf16[128,768]{1,0:T(8,128)(2,1)S(1)}, bf16[128,768]{1,0:T(8,128)(2,1)S(1)}, u32[]{:S(2)}, u32[]{:S(2)}) collective-permute-start(bf16[128,768]{1,0:T(8,128)(2,1)S(1)} %collective-permute-done.29.rest_5_), channel_id=1, source_target_pairs={{0,80},{32,112},{64,0},{96,32},{16,64},{48,96},{80,16},{112,48},{1... | collective-permute-start | bytes 589832 | tf_op jit(solution)/shard_map/ppermute | solution.py:35
  242.5 3.3 %collective-permute-done.30.rest_6_ = bf16[128,768]{1,0:T(8,128)(2,1)S(1)} collective-permute-done((bf16[128,768]{1,0:T(8,128)(2,1)S(1)}, bf16[128,768]{1,0:T(8,128)(2,1)S(1)}, u32[]{:S(2)}, u32[]{:S(2)}) %collective-permute-start.30) | collective-permute-done | bytes 196640 | tf_op jit(solution)/shard_map/ppermute | solution.py:35
  246.0 7.0 %attention.7 = (bf16[128,384]{1,0:T(8,128)(2,1)}, bf16[128,384]{1,0:T(8,128)(2,1)}) custom-call(bf16[128,768]{1,0:T(8,128)(2,1)S(1)} %get-tuple-element.31.rest_0_, bf16[128,768]{1,0:T(8,128)(2,1)S(1)} %get-tuple-element.32.rest_1_, bf16[128,768]{1,0:T(8,128)(2,1)S(1)} %collective-permute-done.26.rest_2_, ...), custom_call_target="tpu_custom_call" | custom-call | flops 1811939328 | bytes 10000000 | tf_op jit(solution)/shard_map/attention/pallas_call | solution.py:205
  254.3 5.3 %collective-permute-start.33 = (bf16[128,384]{1,0:T(8,128)(2,1)}, bf16[128,384]{1,0:T(8,128)(2,1)S(1)}, u32[]{:S(2)}, u32[]{:S(2)}) collective-permute-start(bf16[128,384]{1,0:T(8,128)(2,1)} %get-tuple-element.34), channel_id=1, source_target_pairs={{0,16},{32,48},{16,0},{48,32},{1,17},{33,49},{17,1},{49,33},{2,18}... | collective-permute-start | bytes 294920 | tf_op jit(solution)/shard_map/ppermute | solution.py:35
  261.7 5.5 %all-gather.11.cloned.1.call-done = bf16[64,192,384]{2,1,0:T(8,128)(2,1)} async-done(((bf16[2,192,384]{2,1,0:T(8,128)(2,1)}), bf16[64,192,384]{2,1,0:T(8,128)(2,1)}) %all-gather.11.cloned.1.call-update) | async-done | bytes 9437200 | tf_op jit(solution)/shard_map/all_gather | solution.py:338
  267.3 5.3 %finish.1 = (bf16[128,3072]{1,0:T(8,128)(2,1)S(1)}, bf16[128,3072]{1,0:T(8,128)(2,1)S(1)}) custom-call(bf16[128,384]{1,0:T(8,128)(2,1)} %get-tuple-element.33.a0, bf16[128,384]{1,0:T(8,128)(2,1)S(1)} %collective-permute-done.32.a1, bf16[128,384]{1,0:T(8,128)(2,1)S(1)} %collective-permute-done.33.a2, bf16[128,384]{1,0:T(8,128)(2,1)S(1)} %collective-permute-done.34.a3, ...), custom_call_target="tpu_custom_call" | custom-call | flops 1207959552 | bytes 13000000 | tf_op jit(solution)/shard_map/finish/pallas_call | solution.py:237
  273.8 1.9 collective-permute-done.38
  (135 shorter events, 56.4 us)
Async XLA Ops:
  6.5 130.0 %all-gather.7.cloned.1.call-start = ((), (), s32[]{:S(2)}) async-start(), calls=%async_computation.2 | async-start | bytes 19464192 | tf_op jit(solution)/shard_map/all_gather | solution.py:335
  62.5 147.6 %all-gather.9.cloned.1.call-start = ((), (), s32[]{:S(2)}) async-start(), calls=%async_computation.3 | async-start | bytes 17031168 | tf_op jit(solution)/shard_map/all_gather | solution.py:336
  63.5 203.8 %all-gather.11.cloned.1.call-start = ((), (), s32[]{:S(2)}) async-start(), calls=%async_computation.4 | async-start | bytes 9732096 | tf_op jit(solution)/shard_map/all_gather | solution.py:338
  73.9 28.5 %collective-permute-start = (bf16[128,3072]{1,0:T(8,128)(2,1)}, bf16[128,3072]{1,0:T(8,128)(2,1)}, u32[]{:S(2)}, u32[]{:S(2)}) collective-permute-start(bf16[128,3072]{1,0:T(8,128)(2,1)} %dynamic-slice_bitcast_fusion), channel_id=1, source_target_pairs={{0,80},{32,112},{64,16},{96,48},{16,64},{48,96},{80,0},{112,32},{1... | collective-permute-start | bytes 2359304 | tf_op jit(solution)/shard_map/ppermute | solution.py:35
  76.3 22.5 %collective-permute-start.2 = (f32[2,4,3072]{2,1,0:T(4,128)S(1)}, f32[2,4,3072]{2,1,0:T(4,128)S(1)}, u32[]{:S(2)}, u32[]{:S(2)}) collective-permute-start(f32[2,4,3072]{2,1,0:T(4,128)S(1)} %maximum_select_fusion.1), channel_id=1, source_target_pairs={{0,64},{32,96},{64,16},{96,48},{16,80},{48,112},{80,0},{112,32},{1... | collective-permute-start | bytes 294920 | tf_op jit(solution)/shard_map/ppermute | solution.py:35
  76.4 22.5 %collective-permute-start.3 = (f32[2,4,3072]{2,1,0:T(4,128)S(1)}, f32[2,4,3072]{2,1,0:T(4,128)S(1)}, u32[]{:S(2)}, u32[]{:S(2)}) collective-permute-start(f32[2,4,3072]{2,1,0:T(4,128)S(1)} %maximum_select_fusion.1), channel_id=1, source_target_pairs={{0,16},{32,48},{64,80},{96,112},{16,0},{48,32},{80,64},{112,96},{1... | collective-permute-start | bytes 294920 | tf_op jit(solution)/shard_map/ppermute | solution.py:35
  77.9 21.0 %collective-permute-start.4 = (f32[2,4,3072]{2,1,0:T(4,128)S(1)}, f32[2,4,3072]{2,1,0:T(4,128)S(1)}, u32[]{:S(2)}, u32[]{:S(2)}) collective-permute-start(f32[2,4,3072]{2,1,0:T(4,128)S(1)} %maximum_select_fusion.1), channel_id=1, source_target_pairs={{0,80},{32,112},{64,0},{96,32},{16,64},{48,96},{80,16},{112,48},{1... | collective-permute-start | bytes 294920 | tf_op jit(solution)/shard_map/ppermute | solution.py:35
  142.8 7.5 %collective-permute-start.5 = (bf16[256,384]{1,0:T(8,128)(2,1)S(1)}, bf16[256,384]{1,0:T(8,128)(2,1)S(1)}, u32[]{:S(2)}, u32[]{:S(2)}) collective-permute-start(bf16[256,384]{1,0:T(8,128)(2,1)S(1)} %attention.4.a0), channel_id=1, source_target_pairs={{0,64},{32,96},{64,16},{96,48},{16,80},{48,112},{80,0},{112,32},{1... | collective-permute-start | bytes 589832 | tf_op jit(solution)/shard_map/ppermute | solution.py:35
  144.2 11.6 %collective-permute-start.6 = (bf16[256,384]{1,0:T(8,128)(2,1)S(1)}, bf16[256,384]{1,0:T(8,128)(2,1)S(1)}, u32[]{:S(2)}, u32[]{:S(2)}) collective-permute-start(bf16[256,384]{1,0:T(8,128)(2,1)S(1)} %attention.4.a0), channel_id=1, source_target_pairs={{0,16},{32,48},{64,80},{96,112},{16,0},{48,32},{80,64},{112,96},{1... | collective-permute-start | bytes 589832 | tf_op jit(solution)/shard_map/ppermute | solution.py:35
  146.8 9.0 %collective-permute-start.7 = (bf16[256,384]{1,0:T(8,128)(2,1)S(1)}, bf16[256,384]{1,0:T(8,128)(2,1)S(1)}, u32[]{:S(2)}, u32[]{:S(2)}) collective-permute-start(bf16[256,384]{1,0:T(8,128)(2,1)S(1)} %attention.4.a0), channel_id=1, source_target_pairs={{0,80},{32,112},{64,0},{96,32},{16,64},{48,96},{80,16},{112,48},{1... | collective-permute-start | bytes 589832 | tf_op jit(solution)/shard_map/ppermute | solution.py:35
  156.9 6.7 %collective-permute-start.8 = (bf16[128,768]{1,0:T(8,128)(2,1)S(1)}, bf16[128,768]{1,0:T(8,128)(2,1)S(1)}, u32[]{:S(2)}, u32[]{:S(2)}) collective-permute-start(bf16[128,768]{1,0:T(8,128)(2,1)S(1)} %get-tuple-element.23.rest_0_.hidden0), channel_id=1, source_target_pairs={{0,64},{32,96},{64,16},{96,48},{16,80},{48,112},{80,0},{112,32},{1... | collective-permute-start | bytes 589832 | tf_op jit(solution)/shard_map/ppermute | solution.py:35
  159.6 7.4 %collective-permute-start.10 = (bf16[128,768]{1,0:T(8,128)(2,1)S(1)}, bf16[128,768]{1,0:T(8,128)(2,1)S(1)}, u32[]{:S(2)}, u32[]{:S(2)}) collective-permute-start(bf16[128,768]{1,0:T(8,128)(2,1)S(1)} %get-tuple-element.23.rest_0_.hidden0), channel_id=1, source_target_pairs={{0,80},{32,112},{64,0},{96,32},{16,64},{48,96},{80,16},{112,48},{1... | collective-permute-start | bytes 589832 | tf_op jit(solution)/shard_map/ppermute | solution.py:35
  160.8 6.9 %collective-permute-start.9 = (bf16[128,768]{1,0:T(8,128)(2,1)S(1)}, bf16[128,768]{1,0:T(8,128)(2,1)S(1)}, u32[]{:S(2)}, u32[]{:S(2)}) collective-permute-start(bf16[128,768]{1,0:T(8,128)(2,1)S(1)} %get-tuple-element.24.rest_1_.hidden1), channel_id=1, source_target_pairs={{0,64},{32,96},{64,16},{96,48},{16,80},{48,112},{80,0},{112,32},{1... | collective-permute-start | bytes 589832 | tf_op jit(solution)/shard_map/ppermute | solution.py:35
  163.6 8.4 %collective-permute-start.12 = (bf16[128,768]{1,0:T(8,128)(2,1)S(1)}, bf16[128,768]{1,0:T(8,128)(2,1)S(1)}, u32[]{:S(2)}, u32[]{:S(2)}) collective-permute-start(bf16[128,768]{1,0:T(8,128)(2,1)S(1)} %collective-permute-done.8.rest_2_), channel_id=1, source_target_pairs={{0,64},{32,96},{64,16},{96,48},{16,80},{48,112},{80,0},{112,32},{1... | collective-permute-start | bytes 589832 | tf_op jit(solution)/shard_map/ppermute | solution.py:35
  163.6 8.4 %collective-permute-start.13 = (bf16[128,768]{1,0:T(8,128)(2,1)S(1)}, bf16[128,768]{1,0:T(8,128)(2,1)S(1)}, u32[]{:S(2)}, u32[]{:S(2)}) collective-permute-start(bf16[128,768]{1,0:T(8,128)(2,1)S(1)} %collective-permute-done.11.rest_5_), channel_id=1, source_target_pairs={{0,80},{32,112},{64,0},{96,32},{16,64},{48,96},{80,16},{112,48},{1... | collective-permute-start | bytes 589832 | tf_op jit(solution)/shard_map/ppermute | solution.py:35
  178.6 6.8 %collective-permute-start.14 = (bf16[256,384]{1,0:T(8,128)(2,1)S(1)}, bf16[256,384]{1,0:T(8,128)(2,1)S(1)}, u32[]{:S(2)}, u32[]{:S(2)}) collective-permute-start(bf16[256,384]{1,0:T(8,128)(2,1)S(1)} %get-tuple-element.25.a0), channel_id=1, source_target_pairs={{0,64},{32,96},{64,16},{96,48},{16,80},{48,112},{80,0},{112,32},{1... | collective-permute-start | bytes 589832 | tf_op jit(solution)/shard_map/ppermute | solution.py:35
  179.8 9.2 %collective-permute-start.15 = (bf16[256,384]{1,0:T(8,128)(2,1)S(1)}, bf16[256,384]{1,0:T(8,128)(2,1)S(1)}, u32[]{:S(2)}, u32[]{:S(2)}) collective-permute-start(bf16[256,384]{1,0:T(8,128)(2,1)S(1)} %get-tuple-element.25.a0), channel_id=1, source_target_pairs={{0,16},{32,48},{64,80},{96,112},{16,0},{48,32},{80,64},{112,96},{1... | collective-permute-start | bytes 589832 | tf_op jit(solution)/shard_map/ppermute | solution.py:35
  190.2 7.0 %collective-permute-start.17 = (bf16[128,768]{1,0:T(8,128)(2,1)S(1)}, bf16[128,768]{1,0:T(8,128)(2,1)S(1)}, u32[]{:S(2)}, u32[]{:S(2)}) collective-permute-start(bf16[128,768]{1,0:T(8,128)(2,1)S(1)} %get-tuple-element.27.rest_0_.hidden0), channel_id=1, source_target_pairs={{0,64},{32,96},{64,16},{96,48},{16,80},{48,112},{80,0},{112,32},{1... | collective-permute-start | bytes 589832 | tf_op jit(solution)/shard_map/ppermute | solution.py:35
  193.8 16.3 %collective-permute-start.18 = (bf16[128,768]{1,0:T(8,128)(2,1)S(1)}, bf16[128,768]{1,0:T(8,128)(2,1)S(1)}, u32[]{:S(2)}, u32[]{:S(2)}) collective-permute-start(bf16[128,768]{1,0:T(8,128)(2,1)S(1)} %get-tuple-element.28.rest_1_.hidden1), channel_id=1, source_target_pairs={{0,64},{32,96},{64,16},{96,48},{16,80},{48,112},{80,0},{112,32},{1... | collective-permute-start | bytes 589832 | tf_op jit(solution)/shard_map/ppermute | solution.py:35
  194.8 15.3 %collective-permute-start.19 = (bf16[128,768]{1,0:T(8,128)(2,1)S(1)}, bf16[128,768]{1,0:T(8,128)(2,1)S(1)}, u32[]{:S(2)}, u32[]{:S(2)}) collective-permute-start(bf16[128,768]{1,0:T(8,128)(2,1)S(1)} %get-tuple-element.27.rest_0_.hidden0), channel_id=1, source_target_pairs={{0,80},{32,112},{64,0},{96,32},{16,64},{48,96},{80,16},{112,48},{1... | collective-permute-start | bytes 589832 | tf_op jit(solution)/shard_map/ppermute | solution.py:35
  197.2 12.9 %collective-permute-start.21 = (bf16[128,768]{1,0:T(8,128)(2,1)S(1)}, bf16[128,768]{1,0:T(8,128)(2,1)S(1)}, u32[]{:S(2)}, u32[]{:S(2)}) collective-permute-start(bf16[128,768]{1,0:T(8,128)(2,1)S(1)} %collective-permute-done.17.rest_2_), channel_id=1, source_target_pairs={{0,64},{32,96},{64,16},{96,48},{16,80},{48,112},{80,0},{112,32},{1... | collective-permute-start | bytes 589832 | tf_op jit(solution)/shard_map/ppermute | solution.py:35
  198.6 11.5 %collective-permute-start.22 = (bf16[128,768]{1,0:T(8,128)(2,1)S(1)}, bf16[128,768]{1,0:T(8,128)(2,1)S(1)}, u32[]{:S(2)}, u32[]{:S(2)}) collective-permute-start(bf16[128,768]{1,0:T(8,128)(2,1)S(1)} %collective-permute-done.20.rest_5_), channel_id=1, source_target_pairs={{0,80},{32,112},{64,0},{96,32},{16,64},{48,96},{80,16},{112,48},{1... | collective-permute-start | bytes 589832 | tf_op jit(solution)/shard_map/ppermute | solution.py:35
  217.6 7.5 %collective-permute-start.23 = (bf16[256,384]{1,0:T(8,128)(2,1)S(1)}, bf16[256,384]{1,0:T(8,128)(2,1)S(1)}, u32[]{:S(2)}, u32[]{:S(2)}) collective-permute-start(bf16[256,384]{1,0:T(8,128)(2,1)S(1)} %get-tuple-element.29.a0), channel_id=1, source_target_pairs={{0,64},{32,96},{64,16},{96,48},{16,80},{48,112},{80,0},{112,32},{1... | collective-permute-start | bytes 589832 | tf_op jit(solution)/shard_map/ppermute | solution.py:35
  218.9 11.6 %collective-permute-start.24 = (bf16[256,384]{1,0:T(8,128)(2,1)S(1)}, bf16[256,384]{1,0:T(8,128)(2,1)S(1)}, u32[]{:S(2)}, u32[]{:S(2)}) collective-permute-start(bf16[256,384]{1,0:T(8,128)(2,1)S(1)} %get-tuple-element.29.a0), channel_id=1, source_target_pairs={{0,16},{32,48},{64,80},{96,112},{16,0},{48,32},{80,64},{112,96},{1... | collective-permute-start | bytes 589832 | tf_op jit(solution)/shard_map/ppermute | solution.py:35
  221.5 9.0 %collective-permute-start.25 = (bf16[256,384]{1,0:T(8,128)(2,1)S(1)}, bf16[256,384]{1,0:T(8,128)(2,1)S(1)}, u32[]{:S(2)}, u32[]{:S(2)}) collective-permute-start(bf16[256,384]{1,0:T(8,128)(2,1)S(1)} %get-tuple-element.29.a0), channel_id=1, source_target_pairs={{0,80},{32,112},{64,0},{96,32},{16,64},{48,96},{80,16},{112,48},{1... | collective-permute-start | bytes 589832 | tf_op jit(solution)/shard_map/ppermute | solution.py:35
  234.3 8.2 %collective-permute-start.27 = (bf16[128,768]{1,0:T(8,128)(2,1)S(1)}, bf16[128,768]{1,0:T(8,128)(2,1)S(1)}, u32[]{:S(2)}, u32[]{:S(2)}) collective-permute-start(bf16[128,768]{1,0:T(8,128)(2,1)S(1)} %get-tuple-element.32.rest_1_), channel_id=1, source_target_pairs={{0,64},{32,96},{64,16},{96,48},{16,80},{48,112},{80,0},{112,32},{1... | collective-permute-start | bytes 589832 | tf_op jit(solution)/shard_map/ppermute | solution.py:35
  234.3 8.2 %collective-permute-start.28 = (bf16[128,768]{1,0:T(8,128)(2,1)S(1)}, bf16[128,768]{1,0:T(8,128)(2,1)S(1)}, u32[]{:S(2)}, u32[]{:S(2)}) collective-permute-start(bf16[128,768]{1,0:T(8,128)(2,1)S(1)} %get-tuple-element.31.rest_0_), channel_id=1, source_target_pairs={{0,80},{32,112},{64,0},{96,32},{16,64},{48,96},{80,16},{112,48},{1... | collective-permute-start | bytes 589832 | tf_op jit(solution)/shard_map/ppermute | solution.py:35
  238.2 7.6 %collective-permute-start.30 = (bf16[128,768]{1,0:T(8,128)(2,1)S(1)}, bf16[128,768]{1,0:T(8,128)(2,1)S(1)}, u32[]{:S(2)}, u32[]{:S(2)}) collective-permute-start(bf16[128,768]{1,0:T(8,128)(2,1)S(1)} %collective-permute-done.26.rest_2_), channel_id=1, source_target_pairs={{0,64},{32,96},{64,16},{96,48},{16,80},{48,112},{80,0},{112,32},{1... | collective-permute-start | bytes 589832 | tf_op jit(solution)/shard_map/ppermute | solution.py:35
  238.2 7.8 %collective-permute-start.31 = (bf16[128,768]{1,0:T(8,128)(2,1)S(1)}, bf16[128,768]{1,0:T(8,128)(2,1)S(1)}, u32[]{:S(2)}, u32[]{:S(2)}) collective-permute-start(bf16[128,768]{1,0:T(8,128)(2,1)S(1)} %collective-permute-done.29.rest_5_), channel_id=1, source_target_pairs={{0,80},{32,112},{64,0},{96,32},{16,64},{48,96},{80,16},{112,48},{1... | collective-permute-start | bytes 589832 | tf_op jit(solution)/shard_map/ppermute | solution.py:35
  253.0 14.2 %collective-permute-start.32 = (bf16[128,384]{1,0:T(8,128)(2,1)}, bf16[128,384]{1,0:T(8,128)(2,1)S(1)}, u32[]{:S(2)}, u32[]{:S(2)}) collective-permute-start(bf16[128,384]{1,0:T(8,128)(2,1)} %get-tuple-element.34), channel_id=1, source_target_pairs={{64,16},{96,48},{80,0},{112,32},{65,17},{97,49},{81,1},{113,33},{6... | collective-permute-start | bytes 294920 | tf_op jit(solution)/shard_map/ppermute | solution.py:35
  254.3 12.9 %collective-permute-start.33 = (bf16[128,384]{1,0:T(8,128)(2,1)}, bf16[128,384]{1,0:T(8,128)(2,1)S(1)}, u32[]{:S(2)}, u32[]{:S(2)}) collective-permute-start(bf16[128,384]{1,0:T(8,128)(2,1)} %get-tuple-element.34), channel_id=1, source_target_pairs={{0,16},{32,48},{16,0},{48,32},{1,17},{33,49},{17,1},{49,33},{2,18}... | collective-permute-start | bytes 294920 | tf_op jit(solution)/shard_map/ppermute | solution.py:35
  259.7 7.6 %collective-permute-start.34 = (bf16[128,384]{1,0:T(8,128)(2,1)}, bf16[128,384]{1,0:T(8,128)(2,1)S(1)}, u32[]{:S(2)}, u32[]{:S(2)}) collective-permute-start(bf16[128,384]{1,0:T(8,128)(2,1)} %get-tuple-element.33.a0), channel_id=1, source_target_pairs={{64,0},{96,32},{80,16},{112,48},{65,1},{97,33},{81,17},{113,49},{6... | collective-permute-start | bytes 294920 | tf_op jit(solution)/shard_map/ppermute | solution.py:35
  (20 other events, 111.9 us)
Sparse Core Ops, SparseCore 0:
  62.6 73.8 all-gather.6
  138.8 71.2 all-gather.8
  212.4 54.8 all-gather.10

commit v2 on v1

--- a/solution.py
+++ b/solution.py
@@ -354,10 +354,10 @@
     moves = [(cross, {1: 2, 3: 0}), (cross, {0: 2, 2: 0}), (same, {1: 0, 3: 2})]
     parts = [same] + [device_permute(value, lambda a, c: (move[a], c) if a in move else None) for value, move in moves]
     stay, leave = finish(parts, pieces, last_gate, final, kept)
-    leave = core_swap(leave)
-    first = jnp.where(core == 0, stay, leave)
-    second = jnp.where(core == 0, leave, stay)
-    return jnp.stack([first, second])[None, :, None]
+    arrived = core_swap(leave)
+    out = lax.dynamic_update_slice(jnp.zeros((2, TOK, D), jnp.bfloat16), stay[None], (core, 0, 0))
+    out = lax.dynamic_update_slice(out, arrived[None], (1 - core, 0, 0))
+    return out[None, :, None]
 
 
 def solution(mesh):

time: 289 us -> 289 us (level)
  Pallas kernels: 41.8 us -> 36.5 us
  other arithmetic: 7.19 us -> 11.1 us
    pallas_call x0 -> x1, other arithmetic: none -> 5.4 us  [finish(): pl.pallas_call(finish_kernel, out_shape=(jax.ShapeDtypeStruct((TOK, D), j...]
    pallas_call x1 -> x0, Pallas kernels: 5.34 us -> none  [finish(): pl.pallas_call(finish_kernel, out_shape=(jax.ShapeDtypeStruct((TOK, D), j...]
where the time goes in v2:
time: 289 us; the launch traced here: 284 us
  waiting for transfers between devices  104 us (36%)
  starting transfers between devices  58.4 us (20%)
  blocking collectives  51.4 us (18%)
  Pallas kernels  36.5 us (13%)
  between operations  14 us (5%)
  other arithmetic  11.1 us (4%)
  local copies, waits for them, and re-layouts  8.05 us (3%)
    ppermute x37, starting transfers between devices, device_permute(): return lax.ppermute(value, ('z_lo', 'core', 'z_hi'), pairs)  55.6 us
    ppermute x37, waiting for transfers between devices, device_permute(): return lax.ppermute(value, ('z_lo', 'core', 'z_hi'), pairs)  54 us
    all_gather x1, waiting for transfers between devices, on_device(): lax.all_gather(jnp.concatenate([shards[0], shards[1]], axis=1), plane)  32.6 us
    all_to_all x1, blocking collectives, weight_shards(): mixed = lax.all_to_all(packed, ('z_hi', 'x', 'y'), 0, 0)  30.4 us
    pallas_call x4, Pallas kernels, attention(): pl.pallas_call(functools.partial(attention_kernel, first, keeps, last), o...  26.6 us
    all_to_all x1, blocking collectives, weight_shards(): shards = lax.all_to_all(blocks, ('z_lo', 'core', 'z_hi'), 0, 0)  21 us
    all_gather x1, waiting for transfers between devices, on_device(): lax.all_gather(jnp.concatenate([shards[2], shards[3, :, :144]], axis=1),...  10.2 us
  transfers between devices with their start and end apart: 42, of which 22 were waited for; matrix products, arithmetic and copies ran while one was open for 3% of the time, Pallas kernels for 12%

profile of v2, /device:TPU:1, one launch (start us, length us, event | category | flops | bytes accessed | tf_op | source)
XLA Modules:
  0.0 283.7 jit_solution(8105298811504773189)
XLA Ops:
  9.6 30.4 %all_to_all.10.mixed = bf16[32,48,384]{2,1,0:T(8,128)(2,1)S(1)} all-to-all(bf16[32,48,384]{2,1,0:T(8,128)(2,1)S(1)} %pack.1), channel_id=1, replica_groups=mesh['z_lo'=2,'core'=2,'z_hi'=2,'x'=4,'y'=4] {'z_hi','x','y'}, dimensions={0} | all-to-all | bytes 2359296 | tf_op jit(solution)/shard_map/all_to_all | solution.py:285
  40.5 21.0 %all_to_all.11 = bf16[8,192,384]{2,1,0:T(8,128)(2,1)S(1)} all-to-all(bf16[8,192,384]{2,1,0:T(8,128)(2,1)S(1)} %regroup.1), channel_id=1, replica_groups=mesh['z_lo'=2,'core'=2,'z_hi'=2,'x'=4,'y'=4] {'z_lo','core','z_hi'}, dimensions={0} | all-to-all | bytes 2359296 | tf_op jit(solution)/shard_map/all_to_all | solution.py:292
  66.4 2.4 collective-permute-done.35
  73.9 2.3 collective-permute-start
  79.7 19.1 %collective-permute-done.2 = f32[2,4,3072]{2,1,0:T(4,128)S(1)} collective-permute-done((f32[2,4,3072]{2,1,0:T(4,128)S(1)}, f32[2,4,3072]{2,1,0:T(4,128)S(1)}, u32[]{:S(2)}, u32[]{:S(2)}) %collective-permute-start.2) | collective-permute-done | bytes 98336 | tf_op jit(solution)/shard_map/ppermute | solution.py:35
  103.9 32.6 %all-gather.7.cloned.1.call-done = bf16[64,384,384]{2,1,0:T(8,128)(2,1)} async-done(((bf16[2,384,384]{2,1,0:T(8,128)(2,1)}), bf16[64,384,384]{2,1,0:T(8,128)(2,1)}) %all-gather.7.cloned.1.call-update) | async-done | bytes 18874384 | tf_op jit(solution)/shard_map/all_gather | solution.py:335
  136.5 6.3 %attention.4.a0 = bf16[256,384]{1,0:T(8,128)(2,1)S(1)} custom-call(bf16[128,768]{1,0:T(8,128)(2,1)S(1)} %get-tuple-element.81.rest_0_, bf16[128,768]{1,0:T(8,128)(2,1)S(1)} %get-tuple-element.52.rest_1_, bf16[128,768]{1,0:T(8,128)(2,1)S(1)} %get-tuple-element.82.rest_2_, bf16[128,768]{1,0:T(8,128)(2,1)S(1)} %get-tuple-element.51.rest_3_, ...), custom_call_target="tpu_custom_call" | custom-call | flops 1811939328 | bytes 10000000 | tf_op jit(solution)/shard_map/attention/pallas_call | solution.py:205
  144.2 2.6 collective-permute-start.6
  147.9 1.8 fetch.3.w
  150.4 5.4 %collective-permute-done.6.a2 = bf16[256,384]{1,0:T(8,128)(2,1)S(1)} collective-permute-done((bf16[256,384]{1,0:T(8,128)(2,1)S(1)}, bf16[256,384]{1,0:T(8,128)(2,1)S(1)}, u32[]{:S(2)}, u32[]{:S(2)}) %collective-permute-start.6) | collective-permute-done | bytes 196640 | tf_op jit(solution)/shard_map/ppermute | solution.py:35
  157.8 1.8 collective-permute-start.11
  161.1 2.5 collective-permute-done.8.rest_2_
  163.6 2.7 collective-permute-start.13
  167.7 4.2 %collective-permute-done.12.rest_6_ = bf16[128,768]{1,0:T(8,128)(2,1)S(1)} collective-permute-done((bf16[128,768]{1,0:T(8,128)(2,1)S(1)}, bf16[128,768]{1,0:T(8,128)(2,1)S(1)}, u32[]{:S(2)}, u32[]{:S(2)}) %collective-permute-start.12) | collective-permute-done | bytes 196640 | tf_op jit(solution)/shard_map/ppermute | solution.py:35
  171.9 6.6 %attention.5 = (bf16[256,384]{1,0:T(8,128)(2,1)S(1)}, bf16[128,3072]{1,0:T(8,128)(2,1)S(1)}) custom-call(bf16[128,768]{1,0:T(8,128)(2,1)S(1)} %get-tuple-element.23.rest_0_.hidden0, bf16[128,768]{1,0:T(8,128)(2,1)S(1)} %get-tuple-element.24.rest_1_.hidden1, bf16[128,768]{1,0:T(8,128)(2,1)S(1)} %collective-permute-done.8.rest_2_, ...), custom_call_target="tpu_custom_call" | custom-call | flops 1811939328 | bytes 10000000 | tf_op jit(solution)/shard_map/attention/pallas_call | solution.py:205
  179.8 2.6 collective-permute-start.15
  183.6 1.8 fetch.4.w
  185.4 3.7 %collective-permute-done.15.a2 = bf16[256,384]{1,0:T(8,128)(2,1)S(1)} collective-permute-done((bf16[256,384]{1,0:T(8,128)(2,1)S(1)}, bf16[256,384]{1,0:T(8,128)(2,1)S(1)}, u32[]{:S(2)}, u32[]{:S(2)}) %collective-permute-start.15) | collective-permute-done | bytes 196640 | tf_op jit(solution)/shard_map/ppermute | solution.py:35
  190.2 3.2 %collective-permute-start.17 = (bf16[128,768]{1,0:T(8,128)(2,1)S(1)}, bf16[128,768]{1,0:T(8,128)(2,1)S(1)}, u32[]{:S(2)}, u32[]{:S(2)}) collective-permute-start(bf16[128,768]{1,0:T(8,128)(2,1)S(1)} %get-tuple-element.27.rest_0_.hidden0), channel_id=1, source_target_pairs={{0,64},{32,96},{64,16},{96,48},{16,80},{48,112},{80,0},{112,32},{1... | collective-permute-start | bytes 589832 | tf_op jit(solution)/shard_map/ppermute | solution.py:35
  199.9 10.2 %all-gather.9.cloned.1.call-done = bf16[64,336,384]{2,1,0:T(8,128)(2,1)} async-done(((bf16[2,336,384]{2,1,0:T(8,128)(2,1)}), bf16[64,336,384]{2,1,0:T(8,128)(2,1)}) %all-gather.9.cloned.1.call-update) | async-done | bytes 16515088 | tf_op jit(solution)/shard_map/all_gather | solution.py:336
  210.9 6.6 %attention.6 = (bf16[256,384]{1,0:T(8,128)(2,1)S(1)}, bf16[128,3072]{1,0:T(8,128)(2,1)S(1)}) custom-call(bf16[128,768]{1,0:T(8,128)(2,1)S(1)} %get-tuple-element.27.rest_0_.hidden0, bf16[128,768]{1,0:T(8,128)(2,1)S(1)} %get-tuple-element.28.rest_1_.hidden1, bf16[128,768]{1,0:T(8,128)(2,1)S(1)} %collective-permute-done.17.rest_2_, ...), custom_call_target="tpu_custom_call" | custom-call | flops 1811939328 | bytes 10000000 | tf_op jit(solution)/shard_map/attention/pallas_call | solution.py:205
  218.9 2.6 collective-permute-start.24
  225.1 5.4 %collective-permute-done.24.a2 = bf16[256,384]{1,0:T(8,128)(2,1)S(1)} collective-permute-done((bf16[256,384]{1,0:T(8,128)(2,1)S(1)}, bf16[256,384]{1,0:T(8,128)(2,1)S(1)}, u32[]{:S(2)}, u32[]{:S(2)}) %collective-permute-start.24) | collective-permute-done | bytes 196640 | tf_op jit(solution)/shard_map/ppermute | solution.py:35
  232.5 1.8 collective-permute-start.29
  234.3 2.7 collective-permute-start.28
  238.2 2.9 %collective-permute-start.31 = (bf16[128,768]{1,0:T(8,128)(2,1)S(1)}, bf16[128,768]{1,0:T(8,128)(2,1)S(1)}, u32[]{:S(2)}, u32[]{:S(2)}) collective-permute-start(bf16[128,768]{1,0:T(8,128)(2,1)S(1)} %collective-permute-done.29.rest_5_), channel_id=1, source_target_pairs={{0,80},{32,112},{64,0},{96,32},{16,64},{48,96},{80,16},{112,48},{1... | collective-permute-start | bytes 589832 | tf_op jit(solution)/shard_map/ppermute | solution.py:35
  242.5 3.3 %collective-permute-done.30.rest_6_ = bf16[128,768]{1,0:T(8,128)(2,1)S(1)} collective-permute-done((bf16[128,768]{1,0:T(8,128)(2,1)S(1)}, bf16[128,768]{1,0:T(8,128)(2,1)S(1)}, u32[]{:S(2)}, u32[]{:S(2)}) %collective-permute-start.30) | collective-permute-done | bytes 196640 | tf_op jit(solution)/shard_map/ppermute | solution.py:35
  246.0 7.0 %attention.7 = (bf16[128,384]{1,0:T(8,128)(2,1)}, bf16[128,384]{1,0:T(8,128)(2,1)}) custom-call(bf16[128,768]{1,0:T(8,128)(2,1)S(1)} %get-tuple-element.31.rest_0_, bf16[128,768]{1,0:T(8,128)(2,1)S(1)} %get-tuple-element.32.rest_1_, bf16[128,768]{1,0:T(8,128)(2,1)S(1)} %collective-permute-done.26.rest_2_, ...), custom_call_target="tpu_custom_call" | custom-call | flops 1811939328 | bytes 10000000 | tf_op jit(solution)/shard_map/attention/pallas_call | solution.py:205
  254.3 5.3 %collective-permute-start.33 = (bf16[128,384]{1,0:T(8,128)(2,1)}, bf16[128,384]{1,0:T(8,128)(2,1)S(1)}, u32[]{:S(2)}, u32[]{:S(2)}) collective-permute-start(bf16[128,384]{1,0:T(8,128)(2,1)} %get-tuple-element.34), channel_id=1, source_target_pairs={{0,16},{32,48},{16,0},{48,32},{1,17},{33,49},{17,1},{49,33},{2,18}... | collective-permute-start | bytes 294920 | tf_op jit(solution)/shard_map/ppermute | solution.py:35
  261.7 5.5 %all-gather.11.cloned.1.call-done = bf16[64,192,384]{2,1,0:T(8,128)(2,1)} async-done(((bf16[2,192,384]{2,1,0:T(8,128)(2,1)}), bf16[64,192,384]{2,1,0:T(8,128)(2,1)}) %all-gather.11.cloned.1.call-update) | async-done | bytes 9437200 | tf_op jit(solution)/shard_map/all_gather | solution.py:338
  267.5 5.4 %finish.1 = (bf16[1,2,1,128,3072]{4,3,2,1,0:T(8,128)(2,1)S(1)}, bf16[128,3072]{1,0:T(8,128)(2,1)S(1)}) fusion(bf16[1,2,1,128,3072]{4,3,2,1,0:T(8,128)(2,1)S(1)} %broadcast_in_dim.28, s32[]{:T(128)S(6)} %select_n.117, bf16[128,384]{1,0:T(8,128)(2,1)} %get-tuple-element.33, bf16[128,384]{1,0:T(8,128)(2,1)S(1)} %collective-permute-done.32, ...), kind=kCustom, calls=%fused_computation.1 | custom fusion | flops 1207959552 | bytes 14573572 | tf_op jit(solution)/shard_map/finish/pallas_call | solution.py:237
  274.1 1.9 collective-permute-done.38
  (137 shorter events, 56.1 us)
Async XLA Ops:
  6.5 130.0 %all-gather.7.cloned.1.call-start = ((), (), s32[]{:S(2)}) async-start(), calls=%async_computation.2 | async-start | bytes 19464192 | tf_op jit(solution)/shard_map/all_gather | solution.py:335
  62.5 147.6 %all-gather.9.cloned.1.call-start = ((), (), s32[]{:S(2)}) async-start(), calls=%async_computation.3 | async-start | bytes 17031168 | tf_op jit(solution)/shard_map/all_gather | solution.py:336
  63.5 203.8 %all-gather.11.cloned.1.call-start = ((), (), s32[]{:S(2)}) async-start(), calls=%async_computation.4 | async-start | bytes 9732096 | tf_op jit(solution)/shard_map/all_gather | solution.py:338
  73.9 28.5 %collective-permute-start = (bf16[128,3072]{1,0:T(8,128)(2,1)}, bf16[128,3072]{1,0:T(8,128)(2,1)}, u32[]{:S(2)}, u32[]{:S(2)}) collective-permute-start(bf16[128,3072]{1,0:T(8,128)(2,1)} %dynamic-slice_bitcast_fusion), channel_id=1, source_target_pairs={{0,80},{32,112},{64,16},{96,48},{16,64},{48,96},{80,0},{112,32},{1... | collective-permute-start | bytes 2359304 | tf_op jit(solution)/shard_map/ppermute | solution.py:35
  76.3 22.5 %collective-permute-start.2 = (f32[2,4,3072]{2,1,0:T(4,128)S(1)}, f32[2,4,3072]{2,1,0:T(4,128)S(1)}, u32[]{:S(2)}, u32[]{:S(2)}) collective-permute-start(f32[2,4,3072]{2,1,0:T(4,128)S(1)} %maximum_select_fusion.1), channel_id=1, source_target_pairs={{0,64},{32,96},{64,16},{96,48},{16,80},{48,112},{80,0},{112,32},{1... | collective-permute-start | bytes 294920 | tf_op jit(solution)/shard_map/ppermute | solution.py:35
  76.4 22.5 %collective-permute-start.3 = (f32[2,4,3072]{2,1,0:T(4,128)S(1)}, f32[2,4,3072]{2,1,0:T(4,128)S(1)}, u32[]{:S(2)}, u32[]{:S(2)}) collective-permute-start(f32[2,4,3072]{2,1,0:T(4,128)S(1)} %maximum_select_fusion.1), channel_id=1, source_target_pairs={{0,16},{32,48},{64,80},{96,112},{16,0},{48,32},{80,64},{112,96},{1... | collective-permute-start | bytes 294920 | tf_op jit(solution)/shard_map/ppermute | solution.py:35
  77.9 21.0 %collective-permute-start.4 = (f32[2,4,3072]{2,1,0:T(4,128)S(1)}, f32[2,4,3072]{2,1,0:T(4,128)S(1)}, u32[]{:S(2)}, u32[]{:S(2)}) collective-permute-start(f32[2,4,3072]{2,1,0:T(4,128)S(1)} %maximum_select_fusion.1), channel_id=1, source_target_pairs={{0,80},{32,112},{64,0},{96,32},{16,64},{48,96},{80,16},{112,48},{1... | collective-permute-start | bytes 294920 | tf_op jit(solution)/shard_map/ppermute | solution.py:35
  142.8 7.5 %collective-permute-start.5 = (bf16[256,384]{1,0:T(8,128)(2,1)S(1)}, bf16[256,384]{1,0:T(8,128)(2,1)S(1)}, u32[]{:S(2)}, u32[]{:S(2)}) collective-permute-start(bf16[256,384]{1,0:T(8,128)(2,1)S(1)} %attention.4.a0), channel_id=1, source_target_pairs={{0,64},{32,96},{64,16},{96,48},{16,80},{48,112},{80,0},{112,32},{1... | collective-permute-start | bytes 589832 | tf_op jit(solution)/shard_map/ppermute | solution.py:35
  144.2 11.6 %collective-permute-start.6 = (bf16[256,384]{1,0:T(8,128)(2,1)S(1)}, bf16[256,384]{1,0:T(8,128)(2,1)S(1)}, u32[]{:S(2)}, u32[]{:S(2)}) collective-permute-start(bf16[256,384]{1,0:T(8,128)(2,1)S(1)} %attention.4.a0), channel_id=1, source_target_pairs={{0,16},{32,48},{64,80},{96,112},{16,0},{48,32},{80,64},{112,96},{1... | collective-permute-start | bytes 589832 | tf_op jit(solution)/shard_map/ppermute | solution.py:35
  146.8 9.0 %collective-permute-start.7 = (bf16[256,384]{1,0:T(8,128)(2,1)S(1)}, bf16[256,384]{1,0:T(8,128)(2,1)S(1)}, u32[]{:S(2)}, u32[]{:S(2)}) collective-permute-start(bf16[256,384]{1,0:T(8,128)(2,1)S(1)} %attention.4.a0), channel_id=1, source_target_pairs={{0,80},{32,112},{64,0},{96,32},{16,64},{48,96},{80,16},{112,48},{1... | collective-permute-start | bytes 589832 | tf_op jit(solution)/shard_map/ppermute | solution.py:35
  156.9 6.7 %collective-permute-start.8 = (bf16[128,768]{1,0:T(8,128)(2,1)S(1)}, bf16[128,768]{1,0:T(8,128)(2,1)S(1)}, u32[]{:S(2)}, u32[]{:S(2)}) collective-permute-start(bf16[128,768]{1,0:T(8,128)(2,1)S(1)} %get-tuple-element.23.rest_0_.hidden0), channel_id=1, source_target_pairs={{0,64},{32,96},{64,16},{96,48},{16,80},{48,112},{80,0},{112,32},{1... | collective-permute-start | bytes 589832 | tf_op jit(solution)/shard_map/ppermute | solution.py:35
  159.6 7.4 %collective-permute-start.10 = (bf16[128,768]{1,0:T(8,128)(2,1)S(1)}, bf16[128,768]{1,0:T(8,128)(2,1)S(1)}, u32[]{:S(2)}, u32[]{:S(2)}) collective-permute-start(bf16[128,768]{1,0:T(8,128)(2,1)S(1)} %get-tuple-element.23.rest_0_.hidden0), channel_id=1, source_target_pairs={{0,80},{32,112},{64,0},{96,32},{16,64},{48,96},{80,16},{112,48},{1... | collective-permute-start | bytes 589832 | tf_op jit(solution)/shard_map/ppermute | solution.py:35
  160.8 6.9 %collective-permute-start.9 = (bf16[128,768]{1,0:T(8,128)(2,1)S(1)}, bf16[128,768]{1,0:T(8,128)(2,1)S(1)}, u32[]{:S(2)}, u32[]{:S(2)}) collective-permute-start(bf16[128,768]{1,0:T(8,128)(2,1)S(1)} %get-tuple-element.24.rest_1_.hidden1), channel_id=1, source_target_pairs={{0,64},{32,96},{64,16},{96,48},{16,80},{48,112},{80,0},{112,32},{1... | collective-permute-start | bytes 589832 | tf_op jit(solution)/shard_map/ppermute | solution.py:35
  163.6 8.4 %collective-permute-start.12 = (bf16[128,768]{1,0:T(8,128)(2,1)S(1)}, bf16[128,768]{1,0:T(8,128)(2,1)S(1)}, u32[]{:S(2)}, u32[]{:S(2)}) collective-permute-start(bf16[128,768]{1,0:T(8,128)(2,1)S(1)} %collective-permute-done.8.rest_2_), channel_id=1, source_target_pairs={{0,64},{32,96},{64,16},{96,48},{16,80},{48,112},{80,0},{112,32},{1... | collective-permute-start | bytes 589832 | tf_op jit(solution)/shard_map/ppermute | solution.py:35
  163.6 8.4 %collective-permute-start.13 = (bf16[128,768]{1,0:T(8,128)(2,1)S(1)}, bf16[128,768]{1,0:T(8,128)(2,1)S(1)}, u32[]{:S(2)}, u32[]{:S(2)}) collective-permute-start(bf16[128,768]{1,0:T(8,128)(2,1)S(1)} %collective-permute-done.11.rest_5_), channel_id=1, source_target_pairs={{0,80},{32,112},{64,0},{96,32},{16,64},{48,96},{80,16},{112,48},{1... | collective-permute-start | bytes 589832 | tf_op jit(solution)/shard_map/ppermute | solution.py:35
  178.6 6.8 %collective-permute-start.14 = (bf16[256,384]{1,0:T(8,128)(2,1)S(1)}, bf16[256,384]{1,0:T(8,128)(2,1)S(1)}, u32[]{:S(2)}, u32[]{:S(2)}) collective-permute-start(bf16[256,384]{1,0:T(8,128)(2,1)S(1)} %get-tuple-element.25.a0), channel_id=1, source_target_pairs={{0,64},{32,96},{64,16},{96,48},{16,80},{48,112},{80,0},{112,32},{1... | collective-permute-start | bytes 589832 | tf_op jit(solution)/shard_map/ppermute | solution.py:35
  179.8 9.2 %collective-permute-start.15 = (bf16[256,384]{1,0:T(8,128)(2,1)S(1)}, bf16[256,384]{1,0:T(8,128)(2,1)S(1)}, u32[]{:S(2)}, u32[]{:S(2)}) collective-permute-start(bf16[256,384]{1,0:T(8,128)(2,1)S(1)} %get-tuple-element.25.a0), channel_id=1, source_target_pairs={{0,16},{32,48},{64,80},{96,112},{16,0},{48,32},{80,64},{112,96},{1... | collective-permute-start | bytes 589832 | tf_op jit(solution)/shard_map/ppermute | solution.py:35
  190.2 7.0 %collective-permute-start.17 = (bf16[128,768]{1,0:T(8,128)(2,1)S(1)}, bf16[128,768]{1,0:T(8,128)(2,1)S(1)}, u32[]{:S(2)}, u32[]{:S(2)}) collective-permute-start(bf16[128,768]{1,0:T(8,128)(2,1)S(1)} %get-tuple-element.27.rest_0_.hidden0), channel_id=1, source_target_pairs={{0,64},{32,96},{64,16},{96,48},{16,80},{48,112},{80,0},{112,32},{1... | collective-permute-start | bytes 589832 | tf_op jit(solution)/shard_map/ppermute | solution.py:35
  193.8 16.3 %collective-permute-start.18 = (bf16[128,768]{1,0:T(8,128)(2,1)S(1)}, bf16[128,768]{1,0:T(8,128)(2,1)S(1)}, u32[]{:S(2)}, u32[]{:S(2)}) collective-permute-start(bf16[128,768]{1,0:T(8,128)(2,1)S(1)} %get-tuple-element.28.rest_1_.hidden1), channel_id=1, source_target_pairs={{0,64},{32,96},{64,16},{96,48},{16,80},{48,112},{80,0},{112,32},{1... | collective-permute-start | bytes 589832 | tf_op jit(solution)/shard_map/ppermute | solution.py:35
  194.8 15.3 %collective-permute-start.19 = (bf16[128,768]{1,0:T(8,128)(2,1)S(1)}, bf16[128,768]{1,0:T(8,128)(2,1)S(1)}, u32[]{:S(2)}, u32[]{:S(2)}) collective-permute-start(bf16[128,768]{1,0:T(8,128)(2,1)S(1)} %get-tuple-element.27.rest_0_.hidden0), channel_id=1, source_target_pairs={{0,80},{32,112},{64,0},{96,32},{16,64},{48,96},{80,16},{112,48},{1... | collective-permute-start | bytes 589832 | tf_op jit(solution)/shard_map/ppermute | solution.py:35
  197.2 12.9 %collective-permute-start.21 = (bf16[128,768]{1,0:T(8,128)(2,1)S(1)}, bf16[128,768]{1,0:T(8,128)(2,1)S(1)}, u32[]{:S(2)}, u32[]{:S(2)}) collective-permute-start(bf16[128,768]{1,0:T(8,128)(2,1)S(1)} %collective-permute-done.17.rest_2_), channel_id=1, source_target_pairs={{0,64},{32,96},{64,16},{96,48},{16,80},{48,112},{80,0},{112,32},{1... | collective-permute-start | bytes 589832 | tf_op jit(solution)/shard_map/ppermute | solution.py:35
  198.6 11.5 %collective-permute-start.22 = (bf16[128,768]{1,0:T(8,128)(2,1)S(1)}, bf16[128,768]{1,0:T(8,128)(2,1)S(1)}, u32[]{:S(2)}, u32[]{:S(2)}) collective-permute-start(bf16[128,768]{1,0:T(8,128)(2,1)S(1)} %collective-permute-done.20.rest_5_), channel_id=1, source_target_pairs={{0,80},{32,112},{64,0},{96,32},{16,64},{48,96},{80,16},{112,48},{1... | collective-permute-start | bytes 589832 | tf_op jit(solution)/shard_map/ppermute | solution.py:35
  217.6 7.5 %collective-permute-start.23 = (bf16[256,384]{1,0:T(8,128)(2,1)S(1)}, bf16[256,384]{1,0:T(8,128)(2,1)S(1)}, u32[]{:S(2)}, u32[]{:S(2)}) collective-permute-start(bf16[256,384]{1,0:T(8,128)(2,1)S(1)} %get-tuple-element.29.a0), channel_id=1, source_target_pairs={{0,64},{32,96},{64,16},{96,48},{16,80},{48,112},{80,0},{112,32},{1... | collective-permute-start | bytes 589832 | tf_op jit(solution)/shard_map/ppermute | solution.py:35
  218.9 11.6 %collective-permute-start.24 = (bf16[256,384]{1,0:T(8,128)(2,1)S(1)}, bf16[256,384]{1,0:T(8,128)(2,1)S(1)}, u32[]{:S(2)}, u32[]{:S(2)}) collective-permute-start(bf16[256,384]{1,0:T(8,128)(2,1)S(1)} %get-tuple-element.29.a0), channel_id=1, source_target_pairs={{0,16},{32,48},{64,80},{96,112},{16,0},{48,32},{80,64},{112,96},{1... | collective-permute-start | bytes 589832 | tf_op jit(solution)/shard_map/ppermute | solution.py:35
  221.5 9.0 %collective-permute-start.25 = (bf16[256,384]{1,0:T(8,128)(2,1)S(1)}, bf16[256,384]{1,0:T(8,128)(2,1)S(1)}, u32[]{:S(2)}, u32[]{:S(2)}) collective-permute-start(bf16[256,384]{1,0:T(8,128)(2,1)S(1)} %get-tuple-element.29.a0), channel_id=1, source_target_pairs={{0,80},{32,112},{64,0},{96,32},{16,64},{48,96},{80,16},{112,48},{1... | collective-permute-start | bytes 589832 | tf_op jit(solution)/shard_map/ppermute | solution.py:35
  234.3 8.2 %collective-permute-start.27 = (bf16[128,768]{1,0:T(8,128)(2,1)S(1)}, bf16[128,768]{1,0:T(8,128)(2,1)S(1)}, u32[]{:S(2)}, u32[]{:S(2)}) collective-permute-start(bf16[128,768]{1,0:T(8,128)(2,1)S(1)} %get-tuple-element.32.rest_1_), channel_id=1, source_target_pairs={{0,64},{32,96},{64,16},{96,48},{16,80},{48,112},{80,0},{112,32},{1... | collective-permute-start | bytes 589832 | tf_op jit(solution)/shard_map/ppermute | solution.py:35
  234.3 8.2 %collective-permute-start.28 = (bf16[128,768]{1,0:T(8,128)(2,1)S(1)}, bf16[128,768]{1,0:T(8,128)(2,1)S(1)}, u32[]{:S(2)}, u32[]{:S(2)}) collective-permute-start(bf16[128,768]{1,0:T(8,128)(2,1)S(1)} %get-tuple-element.31.rest_0_), channel_id=1, source_target_pairs={{0,80},{32,112},{64,0},{96,32},{16,64},{48,96},{80,16},{112,48},{1... | collective-permute-start | bytes 589832 | tf_op jit(solution)/shard_map/ppermute | solution.py:35
  238.2 7.6 %collective-permute-start.30 = (bf16[128,768]{1,0:T(8,128)(2,1)S(1)}, bf16[128,768]{1,0:T(8,128)(2,1)S(1)}, u32[]{:S(2)}, u32[]{:S(2)}) collective-permute-start(bf16[128,768]{1,0:T(8,128)(2,1)S(1)} %collective-permute-done.26.rest_2_), channel_id=1, source_target_pairs={{0,64},{32,96},{64,16},{96,48},{16,80},{48,112},{80,0},{112,32},{1... | collective-permute-start | bytes 589832 | tf_op jit(solution)/shard_map/ppermute | solution.py:35
  238.2 7.8 %collective-permute-start.31 = (bf16[128,768]{1,0:T(8,128)(2,1)S(1)}, bf16[128,768]{1,0:T(8,128)(2,1)S(1)}, u32[]{:S(2)}, u32[]{:S(2)}) collective-permute-start(bf16[128,768]{1,0:T(8,128)(2,1)S(1)} %collective-permute-done.29.rest_5_), channel_id=1, source_target_pairs={{0,80},{32,112},{64,0},{96,32},{16,64},{48,96},{80,16},{112,48},{1... | collective-permute-start | bytes 589832 | tf_op jit(solution)/shard_map/ppermute | solution.py:35
  253.0 14.2 %collective-permute-start.32 = (bf16[128,384]{1,0:T(8,128)(2,1)}, bf16[128,384]{1,0:T(8,128)(2,1)S(1)}, u32[]{:S(2)}, u32[]{:S(2)}) collective-permute-start(bf16[128,384]{1,0:T(8,128)(2,1)} %get-tuple-element.34), channel_id=1, source_target_pairs={{64,16},{96,48},{80,0},{112,32},{65,17},{97,49},{81,1},{113,33},{6... | collective-permute-start | bytes 294920 | tf_op jit(solution)/shard_map/ppermute | solution.py:35
  254.3 12.9 %collective-permute-start.33 = (bf16[128,384]{1,0:T(8,128)(2,1)}, bf16[128,384]{1,0:T(8,128)(2,1)S(1)}, u32[]{:S(2)}, u32[]{:S(2)}) collective-permute-start(bf16[128,384]{1,0:T(8,128)(2,1)} %get-tuple-element.34), channel_id=1, source_target_pairs={{0,16},{32,48},{16,0},{48,32},{1,17},{33,49},{17,1},{49,33},{2,18}... | collective-permute-start | bytes 294920 | tf_op jit(solution)/shard_map/ppermute | solution.py:35
  259.7 7.6 %collective-permute-start.34 = (bf16[128,384]{1,0:T(8,128)(2,1)}, bf16[128,384]{1,0:T(8,128)(2,1)S(1)}, u32[]{:S(2)}, u32[]{:S(2)}) collective-permute-start(bf16[128,384]{1,0:T(8,128)(2,1)} %get-tuple-element.33), channel_id=1, source_target_pairs={{64,0},{96,32},{80,16},{112,48},{65,1},{97,33},{81,17},{113,49},{6... | collective-permute-start | bytes 294920 | tf_op jit(solution)/shard_map/ppermute | solution.py:35
  (21 other events, 115.1 us)
Sparse Core Ops, SparseCore 0:
  62.6 73.8 all-gather.6
  138.8 71.2 all-gather.8
  212.4 54.8 all-gather.10

commit v3 on v2

--- a/solution.py
+++ b/solution.py
@@ -171,22 +171,24 @@
     states, (gate, weights, kept1, kept2, stay, leave, w, a, early, sems) = rest[:8], rest[8:]
     copies = []
     for k, ring in enumerate((0, 1, 3, 2)):
-        copies.append(pltpu.make_async_copy(weights.at[:, :, :, pl.ds(ring * 48, 48), :], w.at[k], sems.at[k]))
-        copies[-1].start()
+        for n in range(2):
+            source = weights.at[n, :, :, pl.ds(ring * 48, 48), :]
+            copies.append(pltpu.make_async_copy(source, w.at[k, n], sems.at[2 * k + n]))
+            copies[-1].start()
     for i, kept in enumerate((kept1, kept2)):
 
         @pl.when(lax.axis_index("z_lo") == i)
         def bring(kept=kept):
-            pltpu.make_async_copy(kept, early, sems.at[4]).start()
+            pltpu.make_async_copy(kept, early, sems.at[8]).start()
 
     z_lo, core, b, around, order = places()
     for k, part in enumerate((a0, a1, a2, a3)):
         a[:, pl.ds(pl.multiple_of(around[k] * QH, QH), QH)] = part[...]
-    pltpu.make_async_copy(kept1, early, sems.at[4]).wait()
+    pltpu.make_async_copy(kept1, early, sems.at[8]).wait()
     for k in range(4):
-        copies[k].wait()
         q = order[k]
         for n in range(2):
+            copies[2 * k + n].wait()
             cols = pl.ds(n * QH, QH)
             proj = jnp.dot(a[...], w[k, n].reshape(HD, QH), preferred_element_type=jnp.float32).astype(jnp.bfloat16)
             hidden = jnp.where(b == 0, states[2 * k][:, cols], states[2 * k + 1][:, cols])
@@ -243,7 +245,7 @@
             pltpu.VMEM((4, 2, 16, 2, 48, QH), jnp.bfloat16),
             pltpu.VMEM((TOK, HD), jnp.bfloat16),
             pltpu.VMEM((TOK, D), jnp.bfloat16),
-            pltpu.SemaphoreType.DMA((5,)),
+            pltpu.SemaphoreType.DMA((9,)),
         ],
         compiler_params=pltpu.CompilerParams(vmem_limit_bytes=VMEM_LIMIT),
         cost_estimate=pl.CostEstimate(flops=2 * TOK * HD * D, bytes_accessed=13000000, transcendentals=0),

time: 289 us -> 289 us (level)
  no operation moved by 1% of the time
where the time goes in v3:
time: 289 us; the launch traced here: 284 us
  waiting for transfers between devices  104 us (36%)
  starting transfers between devices  58.4 us (20%)
  blocking collectives  51.4 us (18%)
  Pallas kernels  36.5 us (13%)
  between operations  14 us (5%)
  other arithmetic  11.2 us (4%)
  local copies, waits for them, and re-layouts  8.05 us (3%)
    ppermute x37, starting transfers between devices, device_permute(): return lax.ppermute(value, ('z_lo', 'core', 'z_hi'), pairs)  55.6 us
    ppermute x37, waiting for transfers between devices, device_permute(): return lax.ppermute(value, ('z_lo', 'core', 'z_hi'), pairs)  54 us
    all_gather x1, waiting for transfers between devices, on_device(): lax.all_gather(jnp.concatenate([shards[0], shards[1]], axis=1), plane)  32.6 us
    all_to_all x1, blocking collectives, weight_shards(): mixed = lax.all_to_all(packed, ('z_hi', 'x', 'y'), 0, 0)  30.4 us
    pallas_call x4, Pallas kernels, attention(): pl.pallas_call(functools.partial(attention_kernel, first, keeps, last), o...  26.6 us
    all_to_all x1, blocking collectives, weight_shards(): shards = lax.all_to_all(blocks, ('z_lo', 'core', 'z_hi'), 0, 0)  21 us
    all_gather x1, waiting for transfers between devices, on_device(): lax.all_gather(jnp.concatenate([shards[2], shards[3, :, :144]], axis=1),...  10.2 us
  transfers between devices with their start and end apart: 42, of which 22 were waited for; matrix products, arithmetic and copies ran while one was open for 3% of the time, Pallas kernels for 12%

profile of v3, /device:TPU:1, one launch (start us, length us, event | category | flops | bytes accessed | tf_op | source)
XLA Modules:
  0.0 283.8 jit_solution(8920718770220672484)
XLA Ops:
  9.6 30.4 %all_to_all.10.mixed = bf16[32,48,384]{2,1,0:T(8,128)(2,1)S(1)} all-to-all(bf16[32,48,384]{2,1,0:T(8,128)(2,1)S(1)} %pack.1), channel_id=1, replica_groups=mesh['z_lo'=2,'core'=2,'z_hi'=2,'x'=4,'y'=4] {'z_hi','x','y'}, dimensions={0} | all-to-all | bytes 2359296 | tf_op jit(solution)/shard_map/all_to_all | solution.py:287
  40.5 21.0 %all_to_all.11 = bf16[8,192,384]{2,1,0:T(8,128)(2,1)S(1)} all-to-all(bf16[8,192,384]{2,1,0:T(8,128)(2,1)S(1)} %regroup.1), channel_id=1, replica_groups=mesh['z_lo'=2,'core'=2,'z_hi'=2,'x'=4,'y'=4] {'z_lo','core','z_hi'}, dimensions={0} | all-to-all | bytes 2359296 | tf_op jit(solution)/shard_map/all_to_all | solution.py:294
  66.4 2.4 collective-permute-done.35
  73.9 2.3 collective-permute-start
  79.7 19.1 %collective-permute-done.2 = f32[2,4,3072]{2,1,0:T(4,128)S(1)} collective-permute-done((f32[2,4,3072]{2,1,0:T(4,128)S(1)}, f32[2,4,3072]{2,1,0:T(4,128)S(1)}, u32[]{:S(2)}, u32[]{:S(2)}) %collective-permute-start.2) | collective-permute-done | bytes 98336 | tf_op jit(solution)/shard_map/ppermute | solution.py:35
  103.9 32.6 %all-gather.7.cloned.1.call-done = bf16[64,384,384]{2,1,0:T(8,128)(2,1)} async-done(((bf16[2,384,384]{2,1,0:T(8,128)(2,1)}), bf16[64,384,384]{2,1,0:T(8,128)(2,1)}) %all-gather.7.cloned.1.call-update) | async-done | bytes 18874384 | tf_op jit(solution)/shard_map/all_gather | solution.py:337
  136.5 6.3 %attention.4.a0 = bf16[256,384]{1,0:T(8,128)(2,1)S(1)} custom-call(bf16[128,768]{1,0:T(8,128)(2,1)S(1)} %get-tuple-element.81.rest_0_, bf16[128,768]{1,0:T(8,128)(2,1)S(1)} %get-tuple-element.52.rest_1_, bf16[128,768]{1,0:T(8,128)(2,1)S(1)} %get-tuple-element.82.rest_2_, bf16[128,768]{1,0:T(8,128)(2,1)S(1)} %get-tuple-element.51.rest_3_, ...), custom_call_target="tpu_custom_call" | custom-call | flops 1811939328 | bytes 10000000 | tf_op jit(solution)/shard_map/attention/pallas_call | solution.py:207
  144.2 2.6 collective-permute-start.6
  147.9 1.8 fetch.3.w
  150.4 5.4 %collective-permute-done.6.a2 = bf16[256,384]{1,0:T(8,128)(2,1)S(1)} collective-permute-done((bf16[256,384]{1,0:T(8,128)(2,1)S(1)}, bf16[256,384]{1,0:T(8,128)(2,1)S(1)}, u32[]{:S(2)}, u32[]{:S(2)}) %collective-permute-start.6) | collective-permute-done | bytes 196640 | tf_op jit(solution)/shard_map/ppermute | solution.py:35
  157.8 1.8 collective-permute-start.11
  161.1 2.5 collective-permute-done.8.rest_2_
  163.6 2.7 collective-permute-start.13
  167.7 4.2 %collective-permute-done.12.rest_6_ = bf16[128,768]{1,0:T(8,128)(2,1)S(1)} collective-permute-done((bf16[128,768]{1,0:T(8,128)(2,1)S(1)}, bf16[128,768]{1,0:T(8,128)(2,1)S(1)}, u32[]{:S(2)}, u32[]{:S(2)}) %collective-permute-start.12) | collective-permute-done | bytes 196640 | tf_op jit(solution)/shard_map/ppermute | solution.py:35
  171.9 6.6 %attention.5 = (bf16[256,384]{1,0:T(8,128)(2,1)S(1)}, bf16[128,3072]{1,0:T(8,128)(2,1)S(1)}) custom-call(bf16[128,768]{1,0:T(8,128)(2,1)S(1)} %get-tuple-element.23.rest_0_.hidden0, bf16[128,768]{1,0:T(8,128)(2,1)S(1)} %get-tuple-element.24.rest_1_.hidden1, bf16[128,768]{1,0:T(8,128)(2,1)S(1)} %collective-permute-done.8.rest_2_, ...), custom_call_target="tpu_custom_call" | custom-call | flops 1811939328 | bytes 10000000 | tf_op jit(solution)/shard_map/attention/pallas_call | solution.py:207
  179.8 2.6 collective-permute-start.15
  183.6 1.8 fetch.4.w
  185.4 3.7 %collective-permute-done.15.a2 = bf16[256,384]{1,0:T(8,128)(2,1)S(1)} collective-permute-done((bf16[256,384]{1,0:T(8,128)(2,1)S(1)}, bf16[256,384]{1,0:T(8,128)(2,1)S(1)}, u32[]{:S(2)}, u32[]{:S(2)}) %collective-permute-start.15) | collective-permute-done | bytes 196640 | tf_op jit(solution)/shard_map/ppermute | solution.py:35
  190.2 3.2 %collective-permute-start.17 = (bf16[128,768]{1,0:T(8,128)(2,1)S(1)}, bf16[128,768]{1,0:T(8,128)(2,1)S(1)}, u32[]{:S(2)}, u32[]{:S(2)}) collective-permute-start(bf16[128,768]{1,0:T(8,128)(2,1)S(1)} %get-tuple-element.27.rest_0_.hidden0), channel_id=1, source_target_pairs={{0,64},{32,96},{64,16},{96,48},{16,80},{48,112},{80,0},{112,32},{1... | collective-permute-start | bytes 589832 | tf_op jit(solution)/shard_map/ppermute | solution.py:35
  199.9 10.2 %all-gather.9.cloned.1.call-done = bf16[64,336,384]{2,1,0:T(8,128)(2,1)} async-done(((bf16[2,336,384]{2,1,0:T(8,128)(2,1)}), bf16[64,336,384]{2,1,0:T(8,128)(2,1)}) %all-gather.9.cloned.1.call-update) | async-done | bytes 16515088 | tf_op jit(solution)/shard_map/all_gather | solution.py:338
  210.9 6.6 %attention.6 = (bf16[256,384]{1,0:T(8,128)(2,1)S(1)}, bf16[128,3072]{1,0:T(8,128)(2,1)S(1)}) custom-call(bf16[128,768]{1,0:T(8,128)(2,1)S(1)} %get-tuple-element.27.rest_0_.hidden0, bf16[128,768]{1,0:T(8,128)(2,1)S(1)} %get-tuple-element.28.rest_1_.hidden1, bf16[128,768]{1,0:T(8,128)(2,1)S(1)} %collective-permute-done.17.rest_2_, ...), custom_call_target="tpu_custom_call" | custom-call | flops 1811939328 | bytes 10000000 | tf_op jit(solution)/shard_map/attention/pallas_call | solution.py:207
  218.9 2.6 collective-permute-start.24
  225.1 5.4 %collective-permute-done.24.a2 = bf16[256,384]{1,0:T(8,128)(2,1)S(1)} collective-permute-done((bf16[256,384]{1,0:T(8,128)(2,1)S(1)}, bf16[256,384]{1,0:T(8,128)(2,1)S(1)}, u32[]{:S(2)}, u32[]{:S(2)}) %collective-permute-start.24) | collective-permute-done | bytes 196640 | tf_op jit(solution)/shard_map/ppermute | solution.py:35
  232.5 1.8 collective-permute-start.29
  234.3 2.7 collective-permute-start.28
  238.2 2.9 %collective-permute-start.31 = (bf16[128,768]{1,0:T(8,128)(2,1)S(1)}, bf16[128,768]{1,0:T(8,128)(2,1)S(1)}, u32[]{:S(2)}, u32[]{:S(2)}) collective-permute-start(bf16[128,768]{1,0:T(8,128)(2,1)S(1)} %collective-permute-done.29.rest_5_), channel_id=1, source_target_pairs={{0,80},{32,112},{64,0},{96,32},{16,64},{48,96},{80,16},{112,48},{1... | collective-permute-start | bytes 589832 | tf_op jit(solution)/shard_map/ppermute | solution.py:35
  242.5 3.3 %collective-permute-done.30.rest_6_ = bf16[128,768]{1,0:T(8,128)(2,1)S(1)} collective-permute-done((bf16[128,768]{1,0:T(8,128)(2,1)S(1)}, bf16[128,768]{1,0:T(8,128)(2,1)S(1)}, u32[]{:S(2)}, u32[]{:S(2)}) %collective-permute-start.30) | collective-permute-done | bytes 196640 | tf_op jit(solution)/shard_map/ppermute | solution.py:35
  246.0 7.0 %attention.7 = (bf16[128,384]{1,0:T(8,128)(2,1)}, bf16[128,384]{1,0:T(8,128)(2,1)}) custom-call(bf16[128,768]{1,0:T(8,128)(2,1)S(1)} %get-tuple-element.31.rest_0_, bf16[128,768]{1,0:T(8,128)(2,1)S(1)} %get-tuple-element.32.rest_1_, bf16[128,768]{1,0:T(8,128)(2,1)S(1)} %collective-permute-done.26.rest_2_, ...), custom_call_target="tpu_custom_call" | custom-call | flops 1811939328 | bytes 10000000 | tf_op jit(solution)/shard_map/attention/pallas_call | solution.py:207
  254.3 5.3 %collective-permute-start.33 = (bf16[128,384]{1,0:T(8,128)(2,1)}, bf16[128,384]{1,0:T(8,128)(2,1)S(1)}, u32[]{:S(2)}, u32[]{:S(2)}) collective-permute-start(bf16[128,384]{1,0:T(8,128)(2,1)} %get-tuple-element.34), channel_id=1, source_target_pairs={{0,16},{32,48},{16,0},{48,32},{1,17},{33,49},{17,1},{49,33},{2,18}... | collective-permute-start | bytes 294920 | tf_op jit(solution)/shard_map/ppermute | solution.py:35
  261.7 5.5 %all-gather.11.cloned.1.call-done = bf16[64,192,384]{2,1,0:T(8,128)(2,1)} async-done(((bf16[2,192,384]{2,1,0:T(8,128)(2,1)}), bf16[64,192,384]{2,1,0:T(8,128)(2,1)}) %all-gather.11.cloned.1.call-update) | async-done | bytes 9437200 | tf_op jit(solution)/shard_map/all_gather | solution.py:340
  267.5 5.5 %finish.1 = (bf16[1,2,1,128,3072]{4,3,2,1,0:T(8,128)(2,1)S(1)}, bf16[128,3072]{1,0:T(8,128)(2,1)S(1)}) fusion(bf16[1,2,1,128,3072]{4,3,2,1,0:T(8,128)(2,1)S(1)} %broadcast_in_dim.28, s32[]{:T(128)S(6)} %select_n.117, bf16[128,384]{1,0:T(8,128)(2,1)} %get-tuple-element.33, bf16[128,384]{1,0:T(8,128)(2,1)S(1)} %collective-permute-done.32, ...), kind=kCustom, calls=%fused_computation.1 | custom fusion | flops 1207959552 | bytes 14573572 | tf_op jit(solution)/shard_map/finish/pallas_call | solution.py:239
  274.2 1.9 collective-permute-done.38
  (137 shorter events, 56.1 us)
Async XLA Ops:
  6.5 130.0 %all-gather.7.cloned.1.call-start = ((), (), s32[]{:S(2)}) async-start(), calls=%async_computation.2 | async-start | bytes 19464192 | tf_op jit(solution)/shard_map/all_gather | solution.py:337
  62.5 147.6 %all-gather.9.cloned.1.call-start = ((), (), s32[]{:S(2)}) async-start(), calls=%async_computation.3 | async-start | bytes 17031168 | tf_op jit(solution)/shard_map/all_gather | solution.py:338
  63.5 203.8 %all-gather.11.cloned.1.call-start = ((), (), s32[]{:S(2)}) async-start(), calls=%async_computation.4 | async-start | bytes 9732096 | tf_op jit(solution)/shard_map/all_gather | solution.py:340
  73.9 28.5 %collective-permute-start = (bf16[128,3072]{1,0:T(8,128)(2,1)}, bf16[128,3072]{1,0:T(8,128)(2,1)}, u32[]{:S(2)}, u32[]{:S(2)}) collective-permute-start(bf16[128,3072]{1,0:T(8,128)(2,1)} %dynamic-slice_bitcast_fusion), channel_id=1, source_target_pairs={{0,80},{32,112},{64,16},{96,48},{16,64},{48,96},{80,0},{112,32},{1... | collective-permute-start | bytes 2359304 | tf_op jit(solution)/shard_map/ppermute | solution.py:35
  76.3 22.5 %collective-permute-start.2 = (f32[2,4,3072]{2,1,0:T(4,128)S(1)}, f32[2,4,3072]{2,1,0:T(4,128)S(1)}, u32[]{:S(2)}, u32[]{:S(2)}) collective-permute-start(f32[2,4,3072]{2,1,0:T(4,128)S(1)} %maximum_select_fusion.1), channel_id=1, source_target_pairs={{0,64},{32,96},{64,16},{96,48},{16,80},{48,112},{80,0},{112,32},{1... | collective-permute-start | bytes 294920 | tf_op jit(solution)/shard_map/ppermute | solution.py:35
  76.4 22.5 %collective-permute-start.3 = (f32[2,4,3072]{2,1,0:T(4,128)S(1)}, f32[2,4,3072]{2,1,0:T(4,128)S(1)}, u32[]{:S(2)}, u32[]{:S(2)}) collective-permute-start(f32[2,4,3072]{2,1,0:T(4,128)S(1)} %maximum_select_fusion.1), channel_id=1, source_target_pairs={{0,16},{32,48},{64,80},{96,112},{16,0},{48,32},{80,64},{112,96},{1... | collective-permute-start | bytes 294920 | tf_op jit(solution)/shard_map/ppermute | solution.py:35
  77.9 21.0 %collective-permute-start.4 = (f32[2,4,3072]{2,1,0:T(4,128)S(1)}, f32[2,4,3072]{2,1,0:T(4,128)S(1)}, u32[]{:S(2)}, u32[]{:S(2)}) collective-permute-start(f32[2,4,3072]{2,1,0:T(4,128)S(1)} %maximum_select_fusion.1), channel_id=1, source_target_pairs={{0,80},{32,112},{64,0},{96,32},{16,64},{48,96},{80,16},{112,48},{1... | collective-permute-start | bytes 294920 | tf_op jit(solution)/shard_map/ppermute | solution.py:35
  142.8 7.5 %collective-permute-start.5 = (bf16[256,384]{1,0:T(8,128)(2,1)S(1)}, bf16[256,384]{1,0:T(8,128)(2,1)S(1)}, u32[]{:S(2)}, u32[]{:S(2)}) collective-permute-start(bf16[256,384]{1,0:T(8,128)(2,1)S(1)} %attention.4.a0), channel_id=1, source_target_pairs={{0,64},{32,96},{64,16},{96,48},{16,80},{48,112},{80,0},{112,32},{1... | collective-permute-start | bytes 589832 | tf_op jit(solution)/shard_map/ppermute | solution.py:35
  144.2 11.6 %collective-permute-start.6 = (bf16[256,384]{1,0:T(8,128)(2,1)S(1)}, bf16[256,384]{1,0:T(8,128)(2,1)S(1)}, u32[]{:S(2)}, u32[]{:S(2)}) collective-permute-start(bf16[256,384]{1,0:T(8,128)(2,1)S(1)} %attention.4.a0), channel_id=1, source_target_pairs={{0,16},{32,48},{64,80},{96,112},{16,0},{48,32},{80,64},{112,96},{1... | collective-permute-start | bytes 589832 | tf_op jit(solution)/shard_map/ppermute | solution.py:35
  146.8 9.0 %collective-permute-start.7 = (bf16[256,384]{1,0:T(8,128)(2,1)S(1)}, bf16[256,384]{1,0:T(8,128)(2,1)S(1)}, u32[]{:S(2)}, u32[]{:S(2)}) collective-permute-start(bf16[256,384]{1,0:T(8,128)(2,1)S(1)} %attention.4.a0), channel_id=1, source_target_pairs={{0,80},{32,112},{64,0},{96,32},{16,64},{48,96},{80,16},{112,48},{1... | collective-permute-start | bytes 589832 | tf_op jit(solution)/shard_map/ppermute | solution.py:35
  156.9 6.7 %collective-permute-start.8 = (bf16[128,768]{1,0:T(8,128)(2,1)S(1)}, bf16[128,768]{1,0:T(8,128)(2,1)S(1)}, u32[]{:S(2)}, u32[]{:S(2)}) collective-permute-start(bf16[128,768]{1,0:T(8,128)(2,1)S(1)} %get-tuple-element.23.rest_0_.hidden0), channel_id=1, source_target_pairs={{0,64},{32,96},{64,16},{96,48},{16,80},{48,112},{80,0},{112,32},{1... | collective-permute-start | bytes 589832 | tf_op jit(solution)/shard_map/ppermute | solution.py:35
  159.6 7.4 %collective-permute-start.10 = (bf16[128,768]{1,0:T(8,128)(2,1)S(1)}, bf16[128,768]{1,0:T(8,128)(2,1)S(1)}, u32[]{:S(2)}, u32[]{:S(2)}) collective-permute-start(bf16[128,768]{1,0:T(8,128)(2,1)S(1)} %get-tuple-element.23.rest_0_.hidden0), channel_id=1, source_target_pairs={{0,80},{32,112},{64,0},{96,32},{16,64},{48,96},{80,16},{112,48},{1... | collective-permute-start | bytes 589832 | tf_op jit(solution)/shard_map/ppermute | solution.py:35
  160.8 6.9 %collective-permute-start.9 = (bf16[128,768]{1,0:T(8,128)(2,1)S(1)}, bf16[128,768]{1,0:T(8,128)(2,1)S(1)}, u32[]{:S(2)}, u32[]{:S(2)}) collective-permute-start(bf16[128,768]{1,0:T(8,128)(2,1)S(1)} %get-tuple-element.24.rest_1_.hidden1), channel_id=1, source_target_pairs={{0,64},{32,96},{64,16},{96,48},{16,80},{48,112},{80,0},{112,32},{1... | collective-permute-start | bytes 589832 | tf_op jit(solution)/shard_map/ppermute | solution.py:35
  163.6 8.4 %collective-permute-start.12 = (bf16[128,768]{1,0:T(8,128)(2,1)S(1)}, bf16[128,768]{1,0:T(8,128)(2,1)S(1)}, u32[]{:S(2)}, u32[]{:S(2)}) collective-permute-start(bf16[128,768]{1,0:T(8,128)(2,1)S(1)} %collective-permute-done.8.rest_2_), channel_id=1, source_target_pairs={{0,64},{32,96},{64,16},{96,48},{16,80},{48,112},{80,0},{112,32},{1... | collective-permute-start | bytes 589832 | tf_op jit(solution)/shard_map/ppermute | solution.py:35
  163.6 8.4 %collective-permute-start.13 = (bf16[128,768]{1,0:T(8,128)(2,1)S(1)}, bf16[128,768]{1,0:T(8,128)(2,1)S(1)}, u32[]{:S(2)}, u32[]{:S(2)}) collective-permute-start(bf16[128,768]{1,0:T(8,128)(2,1)S(1)} %collective-permute-done.11.rest_5_), channel_id=1, source_target_pairs={{0,80},{32,112},{64,0},{96,32},{16,64},{48,96},{80,16},{112,48},{1... | collective-permute-start | bytes 589832 | tf_op jit(solution)/shard_map/ppermute | solution.py:35
  178.6 6.8 %collective-permute-start.14 = (bf16[256,384]{1,0:T(8,128)(2,1)S(1)}, bf16[256,384]{1,0:T(8,128)(2,1)S(1)}, u32[]{:S(2)}, u32[]{:S(2)}) collective-permute-start(bf16[256,384]{1,0:T(8,128)(2,1)S(1)} %get-tuple-element.25.a0), channel_id=1, source_target_pairs={{0,64},{32,96},{64,16},{96,48},{16,80},{48,112},{80,0},{112,32},{1... | collective-permute-start | bytes 589832 | tf_op jit(solution)/shard_map/ppermute | solution.py:35
  179.8 9.2 %collective-permute-start.15 = (bf16[256,384]{1,0:T(8,128)(2,1)S(1)}, bf16[256,384]{1,0:T(8,128)(2,1)S(1)}, u32[]{:S(2)}, u32[]{:S(2)}) collective-permute-start(bf16[256,384]{1,0:T(8,128)(2,1)S(1)} %get-tuple-element.25.a0), channel_id=1, source_target_pairs={{0,16},{32,48},{64,80},{96,112},{16,0},{48,32},{80,64},{112,96},{1... | collective-permute-start | bytes 589832 | tf_op jit(solution)/shard_map/ppermute | solution.py:35
  190.2 7.0 %collective-permute-start.17 = (bf16[128,768]{1,0:T(8,128)(2,1)S(1)}, bf16[128,768]{1,0:T(8,128)(2,1)S(1)}, u32[]{:S(2)}, u32[]{:S(2)}) collective-permute-start(bf16[128,768]{1,0:T(8,128)(2,1)S(1)} %get-tuple-element.27.rest_0_.hidden0), channel_id=1, source_target_pairs={{0,64},{32,96},{64,16},{96,48},{16,80},{48,112},{80,0},{112,32},{1... | collective-permute-start | bytes 589832 | tf_op jit(solution)/shard_map/ppermute | solution.py:35
  193.8 16.3 %collective-permute-start.18 = (bf16[128,768]{1,0:T(8,128)(2,1)S(1)}, bf16[128,768]{1,0:T(8,128)(2,1)S(1)}, u32[]{:S(2)}, u32[]{:S(2)}) collective-permute-start(bf16[128,768]{1,0:T(8,128)(2,1)S(1)} %get-tuple-element.28.rest_1_.hidden1), channel_id=1, source_target_pairs={{0,64},{32,96},{64,16},{96,48},{16,80},{48,112},{80,0},{112,32},{1... | collective-permute-start | bytes 589832 | tf_op jit(solution)/shard_map/ppermute | solution.py:35
  194.8 15.3 %collective-permute-start.19 = (bf16[128,768]{1,0:T(8,128)(2,1)S(1)}, bf16[128,768]{1,0:T(8,128)(2,1)S(1)}, u32[]{:S(2)}, u32[]{:S(2)}) collective-permute-start(bf16[128,768]{1,0:T(8,128)(2,1)S(1)} %get-tuple-element.27.rest_0_.hidden0), channel_id=1, source_target_pairs={{0,80},{32,112},{64,0},{96,32},{16,64},{48,96},{80,16},{112,48},{1... | collective-permute-start | bytes 589832 | tf_op jit(solution)/shard_map/ppermute | solution.py:35
  197.2 12.9 %collective-permute-start.21 = (bf16[128,768]{1,0:T(8,128)(2,1)S(1)}, bf16[128,768]{1,0:T(8,128)(2,1)S(1)}, u32[]{:S(2)}, u32[]{:S(2)}) collective-permute-start(bf16[128,768]{1,0:T(8,128)(2,1)S(1)} %collective-permute-done.17.rest_2_), channel_id=1, source_target_pairs={{0,64},{32,96},{64,16},{96,48},{16,80},{48,112},{80,0},{112,32},{1... | collective-permute-start | bytes 589832 | tf_op jit(solution)/shard_map/ppermute | solution.py:35
  198.6 11.5 %collective-permute-start.22 = (bf16[128,768]{1,0:T(8,128)(2,1)S(1)}, bf16[128,768]{1,0:T(8,128)(2,1)S(1)}, u32[]{:S(2)}, u32[]{:S(2)}) collective-permute-start(bf16[128,768]{1,0:T(8,128)(2,1)S(1)} %collective-permute-done.20.rest_5_), channel_id=1, source_target_pairs={{0,80},{32,112},{64,0},{96,32},{16,64},{48,96},{80,16},{112,48},{1... | collective-permute-start | bytes 589832 | tf_op jit(solution)/shard_map/ppermute | solution.py:35
  217.6 7.5 %collective-permute-start.23 = (bf16[256,384]{1,0:T(8,128)(2,1)S(1)}, bf16[256,384]{1,0:T(8,128)(2,1)S(1)}, u32[]{:S(2)}, u32[]{:S(2)}) collective-permute-start(bf16[256,384]{1,0:T(8,128)(2,1)S(1)} %get-tuple-element.29.a0), channel_id=1, source_target_pairs={{0,64},{32,96},{64,16},{96,48},{16,80},{48,112},{80,0},{112,32},{1... | collective-permute-start | bytes 589832 | tf_op jit(solution)/shard_map/ppermute | solution.py:35
  218.9 11.6 %collective-permute-start.24 = (bf16[256,384]{1,0:T(8,128)(2,1)S(1)}, bf16[256,384]{1,0:T(8,128)(2,1)S(1)}, u32[]{:S(2)}, u32[]{:S(2)}) collective-permute-start(bf16[256,384]{1,0:T(8,128)(2,1)S(1)} %get-tuple-element.29.a0), channel_id=1, source_target_pairs={{0,16},{32,48},{64,80},{96,112},{16,0},{48,32},{80,64},{112,96},{1... | collective-permute-start | bytes 589832 | tf_op jit(solution)/shard_map/ppermute | solution.py:35
  221.5 9.0 %collective-permute-start.25 = (bf16[256,384]{1,0:T(8,128)(2,1)S(1)}, bf16[256,384]{1,0:T(8,128)(2,1)S(1)}, u32[]{:S(2)}, u32[]{:S(2)}) collective-permute-start(bf16[256,384]{1,0:T(8,128)(2,1)S(1)} %get-tuple-element.29.a0), channel_id=1, source_target_pairs={{0,80},{32,112},{64,0},{96,32},{16,64},{48,96},{80,16},{112,48},{1... | collective-permute-start | bytes 589832 | tf_op jit(solution)/shard_map/ppermute | solution.py:35
  234.3 8.2 %collective-permute-start.27 = (bf16[128,768]{1,0:T(8,128)(2,1)S(1)}, bf16[128,768]{1,0:T(8,128)(2,1)S(1)}, u32[]{:S(2)}, u32[]{:S(2)}) collective-permute-start(bf16[128,768]{1,0:T(8,128)(2,1)S(1)} %get-tuple-element.32.rest_1_), channel_id=1, source_target_pairs={{0,64},{32,96},{64,16},{96,48},{16,80},{48,112},{80,0},{112,32},{1... | collective-permute-start | bytes 589832 | tf_op jit(solution)/shard_map/ppermute | solution.py:35
  234.3 8.2 %collective-permute-start.28 = (bf16[128,768]{1,0:T(8,128)(2,1)S(1)}, bf16[128,768]{1,0:T(8,128)(2,1)S(1)}, u32[]{:S(2)}, u32[]{:S(2)}) collective-permute-start(bf16[128,768]{1,0:T(8,128)(2,1)S(1)} %get-tuple-element.31.rest_0_), channel_id=1, source_target_pairs={{0,80},{32,112},{64,0},{96,32},{16,64},{48,96},{80,16},{112,48},{1... | collective-permute-start | bytes 589832 | tf_op jit(solution)/shard_map/ppermute | solution.py:35
  238.2 7.6 %collective-permute-start.30 = (bf16[128,768]{1,0:T(8,128)(2,1)S(1)}, bf16[128,768]{1,0:T(8,128)(2,1)S(1)}, u32[]{:S(2)}, u32[]{:S(2)}) collective-permute-start(bf16[128,768]{1,0:T(8,128)(2,1)S(1)} %collective-permute-done.26.rest_2_), channel_id=1, source_target_pairs={{0,64},{32,96},{64,16},{96,48},{16,80},{48,112},{80,0},{112,32},{1... | collective-permute-start | bytes 589832 | tf_op jit(solution)/shard_map/ppermute | solution.py:35
  238.2 7.8 %collective-permute-start.31 = (bf16[128,768]{1,0:T(8,128)(2,1)S(1)}, bf16[128,768]{1,0:T(8,128)(2,1)S(1)}, u32[]{:S(2)}, u32[]{:S(2)}) collective-permute-start(bf16[128,768]{1,0:T(8,128)(2,1)S(1)} %collective-permute-done.29.rest_5_), channel_id=1, source_target_pairs={{0,80},{32,112},{64,0},{96,32},{16,64},{48,96},{80,16},{112,48},{1... | collective-permute-start | bytes 589832 | tf_op jit(solution)/shard_map/ppermute | solution.py:35
  253.0 14.2 %collective-permute-start.32 = (bf16[128,384]{1,0:T(8,128)(2,1)}, bf16[128,384]{1,0:T(8,128)(2,1)S(1)}, u32[]{:S(2)}, u32[]{:S(2)}) collective-permute-start(bf16[128,384]{1,0:T(8,128)(2,1)} %get-tuple-element.34), channel_id=1, source_target_pairs={{64,16},{96,48},{80,0},{112,32},{65,17},{97,49},{81,1},{113,33},{6... | collective-permute-start | bytes 294920 | tf_op jit(solution)/shard_map/ppermute | solution.py:35
  254.3 12.9 %collective-permute-start.33 = (bf16[128,384]{1,0:T(8,128)(2,1)}, bf16[128,384]{1,0:T(8,128)(2,1)S(1)}, u32[]{:S(2)}, u32[]{:S(2)}) collective-permute-start(bf16[128,384]{1,0:T(8,128)(2,1)} %get-tuple-element.34), channel_id=1, source_target_pairs={{0,16},{32,48},{16,0},{48,32},{1,17},{33,49},{17,1},{49,33},{2,18}... | collective-permute-start | bytes 294920 | tf_op jit(solution)/shard_map/ppermute | solution.py:35
  259.7 7.6 %collective-permute-start.34 = (bf16[128,384]{1,0:T(8,128)(2,1)}, bf16[128,384]{1,0:T(8,128)(2,1)S(1)}, u32[]{:S(2)}, u32[]{:S(2)}) collective-permute-start(bf16[128,384]{1,0:T(8,128)(2,1)} %get-tuple-element.33), channel_id=1, source_target_pairs={{64,0},{96,32},{80,16},{112,48},{65,1},{97,33},{81,17},{113,49},{6... | collective-permute-start | bytes 294920 | tf_op jit(solution)/shard_map/ppermute | solution.py:35
  (21 other events, 115.1 us)
Sparse Core Ops, SparseCore 0:
  62.6 73.8 all-gather.6
  138.8 71.2 all-gather.8
  212.4 54.8 all-gather.10
